TPU v7x, 256 devices: a whole 4x4x8 slice. The times are simulated.
256 devices in a mesh: tm: 32 (over z, x_lo, core), doc: 8 (over y, x_hi).
Axes of the slice: x: 4 (x_hi: 2, x_lo: 2; x = x_hi * 2 + x_lo), y: 4, z: 8, core: 2. Of those that a mesh axis runs over, the one named last changes fastest.
Arguments:
- beta: float32 [32, 16384, 128], P('tm', 'doc'), may hold values from -6 to 260
- word_ids: int32 [32, 32, 128], P('tm', 'doc'), may hold values from 0 to 16383
- word_counts: int32 [32, 32, 128], P('tm', 'doc'), may hold values from 1 to 8
- block_slot: int32 [128], replicated, may hold values from 0 to 127, each once
- topic_prior: float32 [128], replicated, may hold values from 0.05 to 0.5
- drift_var: float32 [128], replicated, may hold values from 0.0005 to 0.05
- obs_precision: float32 [32, 128], replicated, may hold values from 0.01 to 4
Outputs:
- smoothed_means: float32 [32, 16384, 128], P('tm', 'doc')
- doc_topics: float32 [32, 32, 128], P('tm', 'doc')
Inputs may be any that keep to these rules, and one draw needn't show every extreme that they name: `block_slot`: each block has its own position.
All inputs are finite; a program needn't handle non-finite values.
Results may differ from a plain program's by a relative error of at most 0.0012.
The roundings to bfloat16 on the way count: a program that leaves them out, or rounds other values in their place, can miss the bound.
Values may be sent and summed in bfloat16 or wider, within the bound.
A program may use at most 192 MiB of HBM per device.

v0:
```python
import jax
import jax.numpy as jnp
from jax import lax
from jax.sharding import PartitionSpec as P

K = 128
BLOCK = 128
EITERS = 4


init_variance = 4.0


def joined(value, axis, combine):
    everything = jax.tree.map(lambda part: lax.all_gather(part, axis), value)
    initial = jax.tree.map(lambda part: part[0], everything)

    def step(k, so_far):
        return combine(so_far, jax.tree.map(lambda part: part[k], everything))

    return lax.fori_loop(1, lax.axis_size(axis), step, initial)


def entering(part, axis, combine, identity, reverse):
    count = lax.axis_size(axis)
    place = lax.axis_index(axis)
    ahead = count - 1 - place if reverse else place
    gathered = jax.tree.map(lambda a: lax.all_gather(a, axis), part)
    state = jax.tree.map(lambda a, e: jnp.zeros_like(a) + jnp.asarray(e, a.dtype), part, identity)

    def one(step, state):
        source = count - 1 - step if reverse else step
        return combine(
            state, jax.tree.map(lambda a: lax.dynamic_index_in_dim(a, source, 0, False), gathered)
        )

    return lax.fori_loop(0, ahead, one, state)


def variance_tables(obs_precision, drift_var):

    def forward_step(prior_var, precision):
        denominator = 1.0 + prior_var * precision
        gain_now = prior_var * precision / denominator
        filt_var = prior_var / denominator
        return (filt_var + drift_var, (gain_now, filt_var))

    start_var = jnp.full(drift_var.shape, init_variance, dtype=jnp.float32)
    last_var, (gains, filt_vars) = lax.scan(forward_step, start_var, obs_precision)

    def backward_step(info_next, precision):
        merged = info_next + precision
        shrink = 1.0 / (1.0 + drift_var * merged)
        info_now = merged * shrink
        return (info_now, (shrink, info_now))

    zero_info = jnp.zeros(drift_var.shape, dtype=jnp.float32)
    last_info, (shrinks, infos) = lax.scan(
        backward_step, zero_info, obs_precision[1:], reverse=True
    )
    shrinks = jnp.concatenate([shrinks, jnp.ones_like(zero_info)[None]], axis=0)
    infos = jnp.concatenate([infos, zero_info[None]], axis=0)
    return (gains, filt_vars, shrinks, infos)


def e_step(looked, word_counts, topic_prior):
    counts_float = word_counts.astype(jnp.float32)
    doc_topics = topic_prior + jnp.sum(counts_float, axis=-1, keepdims=True) / K
    scores = looked.astype(jnp.float32)
    for sweep in range(EITERS):
        resp = jax.nn.softmax(lax.digamma(doc_topics)[..., None, :] + scores, axis=-1)
        doc_topics = topic_prior + jnp.sum(counts_float[..., None] * resp, axis=-2)
    weighted = (counts_float[..., None] * resp).astype(jnp.bfloat16)
    return (doc_topics, weighted)


def combine_normalizer(first_part, second_part):
    peak_value = jnp.maximum(first_part[0], second_part[0])
    summed = first_part[1] * jnp.exp(first_part[0] - peak_value) + second_part[1] * jnp.exp(
        second_part[0] - peak_value
    )
    return (peak_value, summed)


def compose_maps(earlier, later):
    return (later[0] * earlier[0], later[0] * earlier[1] + later[1])


def pick_year(table_all, year_index):
    return lax.dynamic_index_in_dim(table_all, year_index, 0, keepdims=False)


def body(beta, word_ids, word_counts, block_slot, topic_prior, drift_var, obs_precision):
    local_beta = beta[0]
    own_words = local_beta.shape[0]
    topics = local_beta.shape[1]
    local_peak = jnp.max(local_beta, axis=0)
    local_total = jnp.sum(jnp.exp(local_beta - local_peak), axis=0)
    peak_value, total_value = joined((local_peak, local_total), "doc", combine_normalizer)
    table = (local_beta - (peak_value + jnp.log(total_value))).astype(jnp.bfloat16)
    slot_ids = word_ids[0]
    doc_count = slot_ids.shape[0]
    slot_width = slot_ids.shape[1]
    block_count = block_slot.shape[0]
    block_of = slot_ids // BLOCK
    block_match = block_of[..., None] == lax.iota(jnp.int32, block_count)
    columns = jnp.sum(jnp.where(block_match, block_slot, 0), axis=-1) * BLOCK + slot_ids % BLOCK
    flat_columns = columns.reshape(-1)
    slot_total = flat_columns.shape[0]
    piece = lax.all_gather(table, "doc", axis=0, tiled=True)
    inside = (flat_columns >= 0) & (flat_columns < piece.shape[0])
    picked = jnp.take(piece, jnp.clip(flat_columns, 0, piece.shape[0] - 1), axis=0)
    looked = jnp.where(inside[:, None], picked, jnp.zeros_like(picked)).reshape(
        doc_count, slot_width, topics
    )
    doc_topics, weighted = e_step(looked, word_counts[0], topic_prior)
    flat_weighted = weighted.reshape(slot_total, topics)
    row_words = lax.iota(jnp.int32, own_words * lax.axis_size("doc"))
    marks = (row_words[:, None] == flat_columns[None, :]).astype(jnp.bfloat16)
    counts = lax.psum_scatter(
        jnp.dot(marks, flat_weighted, preferred_element_type=jnp.float32).astype(jnp.bfloat16),
        "doc",
        scatter_dimension=0,
        tiled=True,
    ).astype(jnp.float32)
    pseudo = local_beta + jnp.log1p(counts)
    gains, filt_vars, shrinks, infos = variance_tables(obs_precision, drift_var)
    year_index = lax.axis_index("tm")
    years_total = obs_precision.shape[0]
    gain_now = pick_year(gains, year_index)
    filt_now = pick_year(filt_vars, year_index)
    keep_part = 1.0 - gain_now
    push_part = gain_now * pseudo
    identity_map = (jnp.ones_like(keep_part), jnp.zeros_like(push_part))
    before = entering((keep_part, push_part), "tm", compose_maps, identity_map, False)
    filtered = keep_part * before[1] + push_part
    pull_now = jnp.where(year_index == years_total - 1, 0.0, filt_now / (filt_now + drift_var))
    own_term = (1.0 - pull_now) * filtered
    after = entering((pull_now, own_term), "tm", compose_maps, identity_map, True)
    smoothed = pull_now * after[1] + own_term
    return (smoothed[None], doc_topics[None])


def solution(mesh):
    in_specs = (
        P("tm", "doc", None),
        P("tm", "doc", None),
        P("tm", "doc", None),
        P(),
        P(),
        P(),
        P(),
    )
    out_specs = (P("tm", "doc", None), P("tm", "doc", None))
    return jax.shard_map(body, mesh=mesh, in_specs=in_specs, out_specs=out_specs, check_vma=False)
```

profile of v0, /device:TPU:1, one launch (start us, length us, event | category | flops | bytes accessed | tf_op | source)
XLA Modules:
  0.0 713.5 jit_solution(3823221200126398408)
XLA Ops:
  7.2 1.5 reduce_max.53
  8.7 1.5 fusion.7
  10.2 20.5 %all-gather.8 = f32[8,1,128]{2,1,0:T(1,128)S(1)} all-gather(f32[1,1,128]{2,1,0:T(1,128)S(1)} %bitcast.207), channel_id=4, replica_groups=mesh['tm'=32,'doc'=8] {'doc'}, dimensions={0}, use_global_device_ids=true | all-gather | bytes 4608 | tf_op jit(solution)/shard_map/all_gather | solution.py:15
  30.8 14.5 %all-gather.7 = f32[8,1,128]{2,1,0:T(1,128)S(1)} all-gather(f32[1,1,128]{2,1,0:T(1,128)S(1)} %bitcast.205), channel_id=3, replica_groups=mesh['tm'=32,'doc'=8] {'doc'}, dimensions={0}, use_global_device_ids=true | all-gather | bytes 4608 | tf_op jit(solution)/shard_map/all_gather | solution.py:15
  45.6 2.1 fusion.8
  47.7 0.8 convert_reduce_fusion
  49.2 0.9 select_reduce_fusion
  52.3 0.8 select_select_fusion.5
  53.8 78.2 %all-gather.13.cloned.1.call-done = bf16[16384,128]{1,0:T(8,128)(2,1)} async-done(((bf16[2048,128]{1,0:T(8,128)(2,1)}), bf16[16384,128]{1,0:T(8,128)(2,1)}) %all-gather.13.cloned.1.call-update) | async-done | bytes 4194320 | tf_op jit(solution)/shard_map/all_gather | solution.py:110
  131.9 3.8 gather_fusion
  136.7 0.7 select_select_fusion.4
  138.2 0.7 select_select_fusion.3
  139.8 0.7 select_select_fusion.2
  141.3 6.8 fusion.4
  148.2 25.0 %while.61 = (s32[]{:T(128)}, f32[128]{0:T(128)S(1)}, f32[32,128]{1,0:T(8,128)S(1)}, f32[32,128]{1,0:T(8,128)S(1)}, f32[32,128]{1,0:T(8,128)}, /*index=5*/f32[128]{0:T(128)S(1)}, s32[]{:T(128)}, s32[]{:T(128)}) while((s32[]{:T(128)}, f32[128]{0:T(128)S(1)}, f32[32,128]{1,0:T(8,128)S(1)}, f32[32,128]{1,0:T(8,128)S(1)}, ...), condition=%wide.region_1.0_spmd.clone, body=%wide.region_0.0_spmd.clone.sunk | while | flops 771 | bytes 5227 | solution.py:49
  158.4 0.7 fusion.79
  159.2 0.7 fusion.79
  163.8 0.7 fusion.79
  164.6 0.7 fusion.79
  168.5 0.7 fusion.79
  169.3 0.7 fusion.79
  170.9 0.7 fusion.79
  172.4 0.7 fusion.79
  173.2 61.9 %reduce-scatter.2.cloned.1.call-done = bf16[2048,128]{1,0:T(8,128)(2,1)} async-done(((bf16[16384,128]{1,0:T(8,128)(2,1)}), bf16[2048,128]{1,0:T(8,128)(2,1)}) %reduce-scatter.2.cloned.1.call-update) | async-done | bytes 524304 | tf_op jit(solution)/shard_map/reduce_scatter | solution.py:120
  235.2 2.4 fusion.9
  237.7 35.0 %all-gather.6 = f32[32,1,128]{2,1,0:T(1,128)S(1)} all-gather(f32[1,1,128]{2,1,0:T(1,128)S(1)} %get-tuple-element.380), channel_id=1, replica_groups=mesh['tm'=32,'doc'=8] {'tm'}, dimensions={0}, use_global_device_ids=true | all-gather | bytes 16896 | tf_op jit(solution)/shard_map/all_gather | solution.py:28
  272.7 149.7 %all-gather.15.cloned.1.call-done = f32[65536,128]{1,0:T(8,128)} async-done(((f32[2048,128]{1,0:T(8,128)}), f32[65536,128]{1,0:T(8,128)}) %all-gather.15.cloned.1.call-update) | async-done | bytes 33554448 | tf_op jit(solution)/shard_map/all_gather | solution.py:28
  422.4 1.7 while.59
  422.5 1.7 bitcast_add_fusion.7
  424.1 1.1 add_multiply_fusion
  425.3 81.5 %all-gather.5 = f32[32,1,128]{2,1,0:T(1,128)S(1)} all-gather(f32[1,1,128]{2,1,0:T(1,128)S(1)} %bitcast.206), channel_id=2, replica_groups=mesh['tm'=32,'doc'=8] {'tm'}, dimensions={0}, use_global_device_ids=true | all-gather | bytes 16896 | tf_op jit(solution)/shard_map/all_gather | solution.py:28
  507.8 149.0 %all-gather.17.cloned.1.call-done = f32[65536,128]{1,0:T(8,128)} async-done(((f32[2048,128]{1,0:T(8,128)}), f32[65536,128]{1,0:T(8,128)}) %all-gather.17.cloned.1.call-update) | async-done | bytes 33554448 | tf_op jit(solution)/shard_map/all_gather | solution.py:28
  656.9 49.0 %while.60 = (s32[]{:T(128)}, f32[2048,128]{1,0:T(8,128)S(1)}, s32[]{:T(128)}, f32[32,128]{1,0:T(8,128)S(1)}, f32[32,2048,128]{2,1,0:T(8,128)}, /*index=5*/s32[]{:T(128)}, s32[]{:T(128)}, s32[]{:T(128)}, s32[]{:T(128)}) while((s32[]{:T(128)}, f32[2048,128]{1,0:T(8,128)S(1)}, s32[]{:T(128)}, f32[32,128]{1,0:T(8,128)S(1)}, ...), condition=%wide.region_23.24_spmd, body=%wide.region_22.23_spmd.sunk | while | flops 524294 | bytes 3147411 | solution.py:37
  656.9 1.7 bitcast_add_fusion.8
  658.6 1.6 bitcast_add_fusion.8
  660.3 1.6 bitcast_add_fusion.8
  661.9 1.6 bitcast_add_fusion.8
  663.5 1.6 bitcast_add_fusion.8
  665.1 1.6 bitcast_add_fusion.8
  666.8 1.6 bitcast_add_fusion.8
  668.4 1.6 bitcast_add_fusion.8
  670.0 1.6 bitcast_add_fusion.8
  671.7 1.6 bitcast_add_fusion.8
  673.3 1.6 bitcast_add_fusion.8
  674.9 1.6 bitcast_add_fusion.8
  676.5 1.6 bitcast_add_fusion.8
  678.2 1.6 bitcast_add_fusion.8
  679.8 1.6 bitcast_add_fusion.8
  681.4 1.6 bitcast_add_fusion.8
  683.1 1.6 bitcast_add_fusion.8
  684.7 1.6 bitcast_add_fusion.8
  686.3 1.6 bitcast_add_fusion.8
  688.0 1.6 bitcast_add_fusion.8
  689.6 1.6 bitcast_add_fusion.8
  691.2 1.6 bitcast_add_fusion.8
  692.8 1.6 bitcast_add_fusion.8
  694.5 1.6 bitcast_add_fusion.8
  696.1 1.6 bitcast_add_fusion.8
  697.7 1.6 bitcast_add_fusion.8
  699.4 1.6 bitcast_add_fusion.8
  701.0 1.6 bitcast_add_fusion.8
  702.6 1.6 bitcast_add_fusion.8
  704.2 1.6 bitcast_add_fusion.8
  705.9 1.1 add_bitcast_fusion
  (180 shorter events, 27.9 us)
Async XLA Ops:
  7.2 124.8 %all-gather.13.cloned.1.call-start = ((), (), s32[]{:S(2)}) async-start(), calls=%async_computation.1 | async-start | bytes 4718592 | tf_op jit(solution)/shard_map/all_gather | solution.py:110
  47.7 187.5 %reduce-scatter.2.cloned.1.call-start = ((), (), s32[]{:S(2)}) async-start(), calls=%async_computation.2 | async-start | bytes 4718592 | tf_op jit(solution)/shard_map/reduce_scatter | solution.py:120
  141.3 6.9 copy-start.3
  141.3 93.8 %copy-start = (f32[1,2048,128]{2,1,0:T(8,128)S(1)}, f32[1,2048,128]{2,1,0:T(8,128)}, u32[]{:S(2)}) copy-start(f32[1,2048,128]{2,1,0:T(8,128)} %param.15) | copy-start | bytes 3145732
  148.1 274.2 %all-gather.15.cloned.1.call-start = ((), (), s32[]{:S(2)}) async-start(), calls=%async_computation.3 | async-start | bytes 34603008 | tf_op jit(solution)/shard_map/all_gather | solution.py:28
  237.6 419.2 %all-gather.17.cloned.1.call-start = ((), (), s32[]{:S(2)}) async-start(), calls=%async_computation.4 | async-start | bytes 34603008 | tf_op jit(solution)/shard_map/all_gather | solution.py:28
  422.3 1.8 copy-start.2
  422.4 84.8 %copy-start.4 = (f32[128]{0:T(128)S(1)}, f32[128]{0:T(128)}, u32[]{:S(2)}) copy-start(f32[128]{0:T(128)} %param.19) | copy-start | bytes 1540
  656.8 49.0 %copy-start.1 = (f32[2048,128]{1,0:T(8,128)S(1)}, f32[2048,128]{1,0:T(8,128)}, u32[]{:S(2)}) copy-start(f32[2048,128]{1,0:T(8,128)} %add_multiply_fusion) | copy-start | bytes 3145732
Sparse Core Ops, SparseCore 0:
  47.8 84.0 all-gather.12
  148.2 86.8 reduce-scatter.1
  237.8 184.5 all-gather.14
  425.4 231.3 all-gather.16
where the time goes:
time: 717 us; the launch traced here: 713 us
  waiting for transfers between devices  439 us (61%)
  blocking collectives  152 us (21%)
  other arithmetic  94.4 us (13%)
  between operations  14 us (2%)
    all_gather x2, waiting for transfers between devices, entering(): gathered = jax.tree.map(lambda a: lax.all_gather(a, axis), part)  299 us
    all_gather x2, blocking collectives, entering(): gathered = jax.tree.map(lambda a: lax.all_gather(a, axis), part)  116 us
    all_gather x1, waiting for transfers between devices, body(): piece = lax.all_gather(table, 'doc', axis=0, tiled=True)  78.2 us
    reduce_scatter x1, waiting for transfers between devices, body(): lax.psum_scatter(jnp.dot(marks, flat_weighted, preferred_element_type=jnp...  61.9 us
    add x31, other arithmetic, compose_maps(): return (later[0] * earlier[0], later[0] * earlier[1] + later[1])  49.3 us
    all_gather x2, blocking collectives, joined(): everything = jax.tree.map(lambda part: lax.all_gather(part, axis), value)  35 us
    add x32, other arithmetic, forward_step(): return (filt_var + drift_var, (gain_now, filt_var))  22.7 us
  transfers between devices with their start and end apart: 4, of which 4 were waited for; matrix products, arithmetic and copies ran while one was open for 4% of the time, Pallas kernels for 0%

commit v1 on v0

v1 whole, which is shorter than its diff:
```python
import functools

import jax
import jax.numpy as jnp
from jax import lax
from jax.experimental import pallas as pl
from jax.experimental.pallas import tpu as pltpu
from jax.sharding import PartitionSpec as P

K = 128
BLOCK = 128
EITERS = 4
GROUP = 4
CHUNKS = 4
INIT_VAR = 4.0
MESH = pl.DeviceIdType.MESH
LINK = jnp.float32


def exp_digamma(x):
    y = x + 6.0
    inv = 1.0 / y
    inv2 = inv * inv
    series = inv * 0.5 + inv2 * (1.0 / 12.0 - inv2 * (1.0 / 120.0 - inv2 * (1.0 / 252.0 - inv2 * (1.0 / 240.0))))
    steps = 1.0 / x
    for i in range(1, 6):
        steps = steps + 1.0 / (x + float(i))
    return y * jnp.exp(-(series + steps))


def send(src, dst, send_sem, recv_sem, where):
    return pltpu.make_async_remote_copy(
        src_ref=src, dst_ref=dst, send_sem=send_sem, recv_sem=recv_sem, device_id=where, device_id_type=MESH
    )


def front_kernel(
    n_doc,
    beta_ref,
    ids_ref,
    cnt_ref,
    slot_ref,
    prior_ref,
    pseudo_ref,
    topics_ref,
    msg,
    land,
    table,
    expo,
    cbro,
    weighted,
    alpha,
    part,
    sums,
    msg_send,
    msg_recv,
    sum_send,
    sum_recv,
):
    me = lax.axis_index("doc")
    own = beta_ref.shape[0]
    dpd = ids_ref.shape[0]
    docs = dpd * n_doc

    def peers():
        return [(off, lax.rem(me + off, n_doc)) for off in range(1, n_doc)]

    barrier = pltpu.get_barrier_semaphore()
    for _, peer in peers():
        pl.semaphore_signal(barrier, inc=1, device_id={"doc": peer}, device_id_type=MESH)

    ids = ids_ref[...]
    block_of = lax.shift_right_logical(ids, 7)
    inside = jnp.bitwise_and(ids, 127)
    place = jnp.zeros_like(ids)
    for b in range(slot_ref.shape[0]):
        place = jnp.where(block_of == b, slot_ref[b], place)
    columns = (place * BLOCK + inside).astype(jnp.float32)
    beta = beta_ref[...]
    peak = jnp.max(beta, axis=0, keepdims=True)
    total = jnp.sum(jnp.exp(beta - peak), axis=0, keepdims=True)
    msg[...] = jnp.zeros_like(msg)
    msg[0:dpd, :] = columns
    msg[dpd : 2 * dpd, :] = cnt_ref[...].astype(jnp.float32)
    msg[2 * dpd : 2 * dpd + 1, :] = peak
    msg[2 * dpd + 1 : 2 * dpd + 2, :] = total
    land[me] = msg[...]

    pl.semaphore_wait(barrier, n_doc - 1)
    for off, peer in peers():
        send(msg, land.at[me], msg_send.at[off], msg_recv.at[me], {"doc": peer}).start()
    for off, peer in peers():
        send(msg, land.at[peer], msg_send.at[off], msg_recv.at[peer], {"doc": peer}).wait_recv()

    peaks = [land[s, 2 * dpd : 2 * dpd + 1, :] for s in range(n_doc)]
    peak = functools.reduce(jnp.maximum, peaks)
    total = sum(land[s, 2 * dpd + 1 : 2 * dpd + 2, :] * jnp.exp(peaks[s] - peak) for s in range(n_doc))
    table[...] = (beta_ref[...] - (peak + jnp.log(total))).astype(jnp.bfloat16)

    base = (me * own).astype(jnp.float32)
    lanes = lax.broadcasted_iota(jnp.int32, (128, 128), 1).astype(jnp.float32)

    def look_up(s, _):
        rows, scales = [], []
        for i in range(dpd):
            col = jnp.transpose(jnp.broadcast_to(land[s, pl.ds(i, 1), :], (128, 128))) - base
            cnt = jnp.transpose(jnp.broadcast_to(land[s, pl.ds(dpd + i, 1), :], (128, 128)))
            rows.append(
                jnp.concatenate(
                    [(col == lanes + float(128 * j)).astype(jnp.bfloat16) for j in range(own // 128)], axis=1
                )
            )
            scales.append(jnp.where((col >= 0.0) & (col < float(own)), cnt, 0.0))
        marks = jnp.concatenate(rows, axis=0)
        looked = jnp.dot(marks, table[...], preferred_element_type=jnp.float32)
        at = pl.ds(pl.multiple_of(s * dpd * 128, dpd * 128), dpd * 128)
        expo[at, :] = jnp.exp(looked - jnp.max(looked, axis=1, keepdims=True))
        cbro[at, :] = jnp.concatenate(scales, axis=0)
        return 0

    lax.fori_loop(0, n_doc, look_up, 0)

    prior = prior_ref[...]
    for s in range(n_doc):
        start = jnp.sum(land[s, dpd : 2 * dpd, :], axis=1, keepdims=True) / K
        alpha[s] = exp_digamma(prior + start)

    for sweep in range(EITERS):
        last = sweep == EITERS - 1

        def e_step(s, _, last=last):
            for i in range(dpd):
                at = pl.ds(pl.multiple_of((s * dpd + i) * 128, 128), 128)
                scaled = expo[at, :] * alpha[s, pl.ds(i, 1), :]
                ratio = cbro[at, :] * (1.0 / jnp.sum(scaled, axis=1, keepdims=True))
                scaled = scaled * ratio
                if last:
                    weighted[at, :] = scaled.astype(jnp.bfloat16)
                part[sweep, s, pl.ds(i, 1), :] = jnp.sum(scaled, axis=0, keepdims=True)
            return 0

        lax.fori_loop(0, n_doc, e_step, 0)
        if not last:
            sums[sweep, me] = part[sweep]
            for off, peer in peers():
                send(
                    part.at[sweep], sums.at[sweep, me], sum_send.at[sweep, off], sum_recv.at[sweep, me], {"doc": peer}
                ).start()
            for off, peer in peers():
                send(
                    part.at[sweep], sums.at[sweep, peer], sum_send.at[sweep, off], sum_recv.at[sweep, peer], {"doc": peer}
                ).wait_recv()
            whole = sums[sweep, 0]
            for s in range(1, n_doc):
                whole = whole + sums[sweep, s]
            alpha[...] = exp_digamma(prior_ref[...] + whole)
        else:
            sums[sweep, me, 0] = part[sweep, me]
            for off, peer in peers():
                send(
                    part.at[sweep, peer],
                    sums.at[sweep, me, 0],
                    sum_send.at[sweep, off],
                    sum_recv.at[sweep, me],
                    {"doc": peer},
                ).start()

    tile = min(own, 512)

    def count(w, _):
        first = pl.multiple_of(w * tile, tile)
        words = (lax.broadcasted_iota(jnp.int32, (tile, 128), 0) + (first + me * own)).astype(jnp.float32)
        marks = jnp.concatenate(
            [(words == land[s, i : i + 1, :]).astype(jnp.bfloat16) for s in range(n_doc) for i in range(dpd)], axis=1
        )
        counts = jnp.dot(marks, weighted[...], preferred_element_type=jnp.float32)
        pseudo_ref[pl.ds(first, tile), :] = beta_ref[pl.ds(first, tile), :] + jnp.log1p(counts)
        return 0

    lax.fori_loop(0, own // tile, count, 0)

    sweep = EITERS - 1
    for off, peer in peers():
        send(
            part.at[sweep, peer], sums.at[sweep, peer, 0], sum_send.at[sweep, off], sum_recv.at[sweep, peer], {"doc": peer}
        ).wait_recv()
    whole = sums[sweep, 0, 0]
    for s in range(1, n_doc):
        whole = whole + sums[sweep, s, 0]
    topics_ref[...] = prior_ref[...] + whole

    for off, peer in peers():
        send(msg, land.at[me], msg_send.at[off], msg_recv.at[me], {"doc": peer}).wait_send()
        for sweep in range(EITERS - 1):
            send(
                part.at[sweep], sums.at[sweep, me], sum_send.at[sweep, off], sum_recv.at[sweep, me], {"doc": peer}
            ).wait_send()
        sweep = EITERS - 1
        send(
            part.at[sweep, peer], sums.at[sweep, me, 0], sum_send.at[sweep, off], sum_recv.at[sweep, me], {"doc": peer}
        ).wait_send()


def smooth_kernel(
    n_tm,
    pseudo_ref,
    prec_ref,
    drift_ref,
    out_ref,
    gain,
    back,
    share,
    years_in,
    local,
    fore,
    hind,
    fore_in,
    hind_in,
    fore_out,
    hind_out,
    years_out,
    in_send,
    in_recv,
    fore_send,
    fore_recv,
    hind_send,
    hind_recv,
    out_send,
    out_recv,
):
    t = lax.axis_index("tm")
    z = t // GROUP
    q = lax.rem(t, GROUP)
    n_z = n_tm // GROUP
    own = pseudo_ref.shape[0]
    span = own // GROUP
    width = span // CHUNKS

    def mates():
        return [(off, lax.rem(q + off, GROUP)) for off in range(1, GROUP)]

    def mate_id(mate):
        return {"tm": z * GROUP + mate}

    barrier = pltpu.get_barrier_semaphore()
    for _, mate in mates():
        pl.semaphore_signal(barrier, inc=1, device_id=mate_id(mate), device_id_type=MESH)

    @pl.when(z > 0)
    def _():
        pl.semaphore_signal(barrier, inc=1, device_id={"tm": t - GROUP}, device_id_type=MESH)

    @pl.when(z < n_z - 1)
    def _():
        pl.semaphore_signal(barrier, inc=1, device_id={"tm": t + GROUP}, device_id_type=MESH)

    pl.semaphore_wait(barrier, GROUP - 1 + jnp.minimum(z, 1) + jnp.minimum(n_z - 1 - z, 1))

    def in_copy(c, off, mate, source):
        return send(
            pseudo_ref.at[pl.ds(pl.multiple_of(mate * span + c * width, width), width), :],
            years_in.at[c, source],
            in_send.at[c, off],
            in_recv.at[c, source],
            mate_id(mate),
        )

    for c in range(CHUNKS):
        for off, mate in mates():
            in_copy(c, off, mate, q).start()

    drift = drift_ref[...]
    var = jnp.full_like(drift, INIT_VAR)
    filt = []
    for k in range(n_tm):
        precision = prec_ref[k : k + 1, :]
        inverse = 1.0 / (1.0 + var * precision)
        gain[k : k + 1, :] = var * precision * inverse
        filt.append(var * inverse)
        var = filt[k] + drift
    info = jnp.zeros_like(drift)
    for k in reversed(range(n_tm)):
        share[k : k + 1, :] = 1.0 / (1.0 + filt[k] * info)
        precision = prec_ref[k : k + 1, :]
        merged = info + precision
        back[k : k + 1, :] = precision / merged
        info = merged / (1.0 + drift * merged)

    g = [gain[pl.ds(z * GROUP + i, 1), :] for i in range(GROUP)]
    r = [back[pl.ds(z * GROUP + i, 1), :] for i in range(GROUP)]
    w = [share[pl.ds(z * GROUP + i, 1), :] for i in range(GROUP)]
    keep = []
    for i in range(GROUP):
        keep.append((1.0 - g[i]) * keep[-1] if i else 1.0 - g[i])
    hold = [jnp.ones_like(g[0])]
    for i in reversed(range(GROUP)):
        hold.insert(0, (1.0 - r[i]) * hold[0])

    def fore_copy(c):
        return send(fore_out.at[c], fore_in.at[c], fore_send.at[c], fore_recv.at[c], {"tm": t + GROUP})

    def hind_copy(c):
        return send(hind_out.at[c], hind_in.at[c], hind_send.at[c], hind_recv.at[c], {"tm": t - GROUP})

    def fore_arrived(c):
        send(fore_out.at[c], fore_in.at[c], fore_send.at[c], fore_recv.at[c], {"tm": t - GROUP}).wait_recv()

    def hind_arrived(c):
        send(hind_out.at[c], hind_in.at[c], hind_send.at[c], hind_recv.at[c], {"tm": t + GROUP}).wait_recv()

    for c in range(CHUNKS):
        years_in[c, q] = pseudo_ref[pl.ds(pl.multiple_of(q * span + c * width, width), width), :].astype(LINK)
        for off, mate in mates():
            in_copy(c, off, mate, mate).wait_recv()
        values = [years_in[c, i].astype(jnp.float32) for i in range(GROUP)]
        ahead = []
        for i in range(GROUP):
            ahead.append(g[i] * values[i] + ((1.0 - g[i]) * ahead[-1] if i else 0.0))
        fore[c] = ahead[-1]
        behind = r[GROUP - 1] * values[GROUP - 1]
        local[c, GROUP - 1] = w[GROUP - 1] * ahead[GROUP - 1]
        for i in reversed(range(GROUP - 1)):
            local[c, i] = w[i] * ahead[i] + (1.0 - w[i]) * behind
            behind = r[i] * values[i] + (1.0 - r[i]) * behind
        hind[c] = behind

        @pl.when(z == 0)
        def _():
            fore_in[c] = jnp.zeros_like(fore_in.at[c])
            fore_out[c] = fore[c].astype(LINK)
            fore_copy(c).start()

        @pl.when(z == n_z - 1)
        def _():
            hind_in[c] = jnp.zeros_like(hind_in.at[c])
            hind_out[c] = hind[c].astype(LINK)
            hind_copy(c).start()

    def do_fore(c):
        @pl.when(z > 0)
        def _():
            fore_arrived(c)

        @pl.when((z > 0) & (z < n_z - 1))
        def _():
            fore_out[c] = (keep[-1] * fore_in[c].astype(jnp.float32) + fore[c]).astype(LINK)
            fore_copy(c).start()

    def do_hind(c):
        @pl.when(z < n_z - 1)
        def _():
            hind_arrived(c)

        @pl.when((z > 0) & (z < n_z - 1))
        def _():
            hind_out[c] = (hold[0] * hind_in[c].astype(jnp.float32) + hind[c]).astype(LINK)
            hind_copy(c).start()

    def out_rows(source, c):
        return pl.ds(pl.multiple_of(source * span + c * width, width), width)

    def out_copy(c, off, mate, source):
        return send(
            years_out.at[c, mate], out_ref.at[out_rows(source, c), :], out_send.at[c, off], out_recv.at[c, source], mate_id(mate)
        )

    def finish(c):
        ahead = fore_in[c].astype(jnp.float32)
        behind = hind_in[c].astype(jnp.float32)
        for i in range(GROUP):
            years_out[c, i] = local[c, i] + (w[i] * keep[i]) * ahead + ((1.0 - w[i]) * hold[i + 1]) * behind
        for off, mate in mates():
            out_copy(c, off, mate, q).start()
        out_ref[out_rows(q, c), :] = years_out[c, q]

    early = z < n_z // 2
    lead = jnp.where(early, n_z - 1 - 2 * z, 2 * z + 1 - n_z)

    def step(k, _):
        @pl.when(k < CHUNKS)
        def _():
            @pl.when(early)
            def _():
                do_fore(k)

            @pl.when(jnp.logical_not(early))
            def _():
                do_hind(k)

        late = k - lead

        @pl.when(late >= 0)
        def _():
            @pl.when(early)
            def _():
                do_hind(late)

            @pl.when(jnp.logical_not(early))
            def _():
                do_fore(late)

            finish(late)

        return 0

    lax.fori_loop(0, CHUNKS + lead, step, 0)

    for c in range(CHUNKS):
        for off, mate in mates():
            out_copy(c, off, mate, mate).wait_recv()
    for c in range(CHUNKS):
        for off, mate in mates():
            in_copy(c, off, mate, q).wait_send()
            out_copy(c, off, mate, q).wait_send()

        @pl.when(z < n_z - 1)
        def _():
            fore_copy(c).wait_send()

        @pl.when(z > 0)
        def _():
            hind_copy(c).wait_send()


def vmem():
    return pl.BlockSpec(memory_space=pltpu.VMEM)


def solution(mesh):
    n_tm, n_doc = mesh.shape["tm"], mesh.shape["doc"]

    def body(beta, word_ids, word_counts, block_slot, topic_prior, drift_var, obs_precision):
        local_beta, ids, cnt = beta[0], word_ids[0], word_counts[0]
        own, dpd = local_beta.shape[0], ids.shape[0]
        slots = dpd * n_doc * 128
        f32, bf16 = jnp.float32, jnp.bfloat16
        dma = pltpu.SemaphoreType.DMA
        pseudo, doc_topics = pl.pallas_call(
            functools.partial(front_kernel, n_doc),
            out_shape=(jax.ShapeDtypeStruct((own, K), f32), jax.ShapeDtypeStruct((dpd, K), f32)),
            in_specs=[vmem(), vmem(), vmem(), pl.BlockSpec(memory_space=pltpu.SMEM), vmem()],
            out_specs=(vmem(), vmem()),
            scratch_shapes=[
                pltpu.VMEM((16, K), f32),
                pltpu.VMEM((n_doc, 16, K), f32),
                pltpu.VMEM((own, K), bf16),
                pltpu.VMEM((slots, K), f32),
                pltpu.VMEM((slots, K), f32),
                pltpu.VMEM((slots, K), bf16),
                pltpu.VMEM((n_doc, dpd, K), f32),
                pltpu.VMEM((EITERS, n_doc, dpd, K), f32),
                pltpu.VMEM((EITERS, n_doc, n_doc, dpd, K), f32),
                dma((n_doc,)),
                dma((n_doc,)),
                dma((EITERS, n_doc)),
                dma((EITERS, n_doc)),
            ],
            compiler_params=pltpu.CompilerParams(
                collective_id=0, has_side_effects=True, vmem_limit_bytes=48 * 1024 * 1024
            ),
            name="estep",
        )(local_beta, ids, cnt, block_slot, topic_prior[None])
        width = own // GROUP // CHUNKS
        smoothed = pl.pallas_call(
            functools.partial(smooth_kernel, n_tm),
            out_shape=jax.ShapeDtypeStruct((own, K), f32),
            in_specs=[vmem(), vmem(), vmem()],
            out_specs=vmem(),
            scratch_shapes=[
                pltpu.VMEM((n_tm, K), f32),
                pltpu.VMEM((n_tm, K), f32),
                pltpu.VMEM((n_tm, K), f32),
                pltpu.VMEM((CHUNKS, GROUP, width, K), LINK),
                pltpu.VMEM((CHUNKS, GROUP, width, K), f32),
                pltpu.VMEM((CHUNKS, width, K), f32),
                pltpu.VMEM((CHUNKS, width, K), f32),
                pltpu.VMEM((CHUNKS, width, K), LINK),
                pltpu.VMEM((CHUNKS, width, K), LINK),
                pltpu.VMEM((CHUNKS, width, K), LINK),
                pltpu.VMEM((CHUNKS, width, K), LINK),
                pltpu.VMEM((CHUNKS, GROUP, width, K), LINK),
                dma((CHUNKS, GROUP)),
                dma((CHUNKS, GROUP)),
                dma((CHUNKS,)),
                dma((CHUNKS,)),
                dma((CHUNKS,)),
                dma((CHUNKS,)),
                dma((CHUNKS, GROUP)),
                dma((CHUNKS, GROUP)),
            ],
            compiler_params=pltpu.CompilerParams(
                collective_id=1, has_side_effects=True, vmem_limit_bytes=48 * 1024 * 1024
            ),
            name="smooth",
        )(pseudo, obs_precision, drift_var[None])
        return (smoothed[None], doc_topics[None])

    in_specs = (P("tm", "doc", None), P("tm", "doc", None), P("tm", "doc", None), P(), P(), P(), P())
    out_specs = (P("tm", "doc", None), P("tm", "doc", None))
    return jax.shard_map(body, mesh=mesh, in_specs=in_specs, out_specs=out_specs, check_vma=False)
```

time: 717 us -> 100 us (0.14)
  waiting for transfers between devices: 439 us -> 0 us
  blocking collectives: 152 us -> 0 us
  Pallas kernels: 0 us -> 95.4 us
  other arithmetic: 94.4 us -> 0 us
  between operations: 14 us -> 0.7 us
    all_gather x3 -> x0, waiting for transfers between devices: 377 us -> none  [the longest x2 299 us: entering(): gathered = jax.tree.map(lambda a: lax.all_gather(a, axis), part)]
    all_gather x4 -> x0, blocking collectives: 152 us -> none  [the longest x2 116 us: entering(): gathered = jax.tree.map(lambda a: lax.all_gather(a, axis), part)]
    pallas_call x0 -> x2, Pallas kernels: none -> 95.4 us  [the longest x1 54.2 us: body(): pl.pallas_call(functools.partial(smooth_kernel, n_tm), out_shape=jax.Shap...]
    add x72 -> x0, other arithmetic: 72.7 us -> none  [the longest x31 49.3 us: compose_maps(): return (later[0] * earlier[0], later[0] * earlier[1] + later[1])]
    reduce_scatter x1 -> x0, waiting for transfers between devices: 61.9 us -> none  [body(): lax.psum_scatter(jnp.dot(marks, flat_weighted, preferred_element_type=jnp...]
  transfers between devices with their start and end apart: 4 -> 0, of which waited for: 4 -> 0; matrix products, arithmetic and copies ran while one was open for 4% -> 0% of each run, Pallas kernels for 0% -> 0%
where the time goes in v1:
time: 100 us
  Pallas kernels  95.4 us (95%)
  local copies, waits for them, and re-layouts  4.09 us (4%)
    pallas_call x1, Pallas kernels, body(): pl.pallas_call(functools.partial(smooth_kernel, n_tm), out_shape=jax.Shap...  54.2 us
    pallas_call x1, Pallas kernels, body(): pl.pallas_call(functools.partial(front_kernel, n_doc), out_shape=(jax.Sha...  41.2 us
    unnamed x16, local copies, waits for them, and re-layouts  4.09 us

profile of v1, /device:TPU:1, one launch (start us, length us, event | category | flops | bytes accessed | tf_op | source)
XLA Modules:
  0.0 100.2 jit_solution(1852164945926249021)
XLA Ops:
  0.6 0.0 copy-start.3
  0.6 0.0 copy-start.2
  0.7 0.0 copy-start.4
  0.7 0.0 copy-start.5
  0.7 0.6 copy-done.3
  1.3 0.0 copy-done.2
  1.3 0.0 copy-done.4
  1.3 0.0 copy-done.5
  1.3 0.0 copy-start
  1.3 1.2 %copy-done = f32[1,2048,128]{2,1,0:T(8,128)S(1)} copy-done((f32[1,2048,128]{2,1,0:T(8,128)S(1)}, f32[1,2048,128]{2,1,0:T(8,128)}, u32[]{:S(2)}) %copy-start) | copy-done | bytes 1048600
  2.6 0.0 copy-start.1
  2.6 41.2 %estep.1 = (f32[2048,128]{1,0:T(8,128)S(1)}, f32[4,128]{1,0:T(4,128)S(1)}) custom-call(f32[2048,128]{1,0:T(8,128)S(1)} %bitcast.8, s32[4,128]{1,0:T(4,128)S(1)} %bitcast.9, s32[4,128]{1,0:T(4,128)S(1)} %bitcast.10, s32[128]{0:T(128)S(1)} %copy-done.4, f32[1,128]{1,0:T(1,128)S(1)} %bitcast.12), custom_call_target="tpu_custom_call" | custom-call | tf_op jit(solution)/shard_map/estep/pallas_call | solution.py:438
  43.7 0.0 copy-start.6
  43.8 0.0 copy-done.1
  43.8 0.6 copy-done.6
  44.4 54.2 %smooth.1 = f32[2048,128]{1,0:T(8,128)S(1)} custom-call(f32[2048,128]{1,0:T(8,128)S(1)} %get-tuple-element.4.pseudo_ref, f32[32,128]{1,0:T(8,128)S(1)} %copy-done.1, f32[1,128]{1,0:T(1,128)S(1)} %bitcast.13), custom_call_target="tpu_custom_call" | custom-call | tf_op jit(solution)/shard_map/smooth/pallas_call | solution.py:464
  98.7 1.0 copy.11
  99.6 0.6 copy.12
Async XLA Ops:
  0.6 0.7 copy-start.3
  0.6 0.7 copy-start.2
  0.7 0.7 copy-start.4
  0.7 0.7 copy-start.5
  1.3 1.2 %copy-start = (f32[1,2048,128]{2,1,0:T(8,128)S(1)}, f32[1,2048,128]{2,1,0:T(8,128)}, u32[]{:S(2)}) copy-start(f32[1,2048,128]{2,1,0:T(8,128)} %param.7) | copy-start | bytes 3145732
  2.6 41.2 %copy-start.1 = (f32[32,128]{1,0:T(8,128)S(1)}, f32[32,128]{1,0:T(8,128)}, u32[]{:S(2)}) copy-start(f32[32,128]{1,0:T(8,128)} %prec_ref.1) | copy-start | bytes 49156
  43.7 0.7 copy-start.6

commit v2 on v0

v2 whole, which is shorter than its diff:
```python
import functools

import jax
import jax.numpy as jnp
from jax import lax
from jax.experimental import pallas as pl
from jax.experimental.pallas import tpu as pltpu
from jax.sharding import PartitionSpec as P

K = 128
BLOCK = 128
EITERS = 4
GROUP = 8
CHUNKS = 2
INIT_VAR = 4.0
MESH = pl.DeviceIdType.MESH


def exp_digamma(x):
    u = x * (x + 5.0)
    steps = (2.0 * x + 5.0) * ((3.0 * u + 20.0) * u + 24.0) / (u * (u + 4.0) * (u + 6.0))
    y = x + 6.0
    inv = 1.0 / y
    inv2 = inv * inv
    series = inv * 0.5 + inv2 * (1.0 / 12.0 - inv2 * (1.0 / 120.0 - inv2 * (1.0 / 252.0 - inv2 * (1.0 / 240.0))))
    return y * jnp.exp(-(series + steps))


def send(src, dst, send_sem, recv_sem, where):
    return pltpu.make_async_remote_copy(
        src_ref=src, dst_ref=dst, send_sem=send_sem, recv_sem=recv_sem, device_id=where, device_id_type=MESH
    )


def kernel(
    n_tm,
    n_doc,
    beta_ref,
    ids_ref,
    cnt_ref,
    slot_ref,
    prior_ref,
    prec_ref,
    drift_ref,
    out_ref,
    topics_ref,
    msg,
    land,
    table,
    rows_out,
    rows_in,
    expo,
    weighted,
    counts,
    gain,
    back,
    share,
    pseudo,
    years_in,
    local,
    mid_out,
    mid_in,
    years_out,
    msg_send,
    msg_recv,
    row_send,
    row_recv,
    wgt_send,
    wgt_recv,
    in_send,
    in_recv,
    mid_send,
    mid_recv,
    out_send,
    out_recv,
):
    me = lax.axis_index("doc")
    t = lax.axis_index("tm")
    n_blocks = n_tm // GROUP
    b = t // GROUP
    m = lax.rem(t, GROUP)
    own = beta_ref.shape[0]
    dpd = ids_ref.shape[0]
    held = dpd * 128
    span = own // GROUP
    width = span // CHUNKS

    peers = [(off, lax.rem(me + off, n_doc)) for off in range(1, n_doc)]
    mates = [(off, lax.rem(m + off, GROUP)) for off in range(1, GROUP)]
    others = [(off, lax.rem(b + off, n_blocks)) for off in range(1, n_blocks)]

    def mate_id(mate):
        return {"tm": b * GROUP + mate}

    def other_id(other):
        return {"tm": other * GROUP + m}

    barrier = pltpu.get_barrier_semaphore()
    for _, peer in peers:
        pl.semaphore_signal(barrier, inc=1, device_id={"doc": peer}, device_id_type=MESH)
    for _, mate in mates:
        pl.semaphore_signal(barrier, inc=1, device_id=mate_id(mate), device_id_type=MESH)
    for _, other in others:
        pl.semaphore_signal(barrier, inc=1, device_id=other_id(other), device_id_type=MESH)

    ids = ids_ref[...]
    block_of = lax.shift_right_logical(ids, 7)
    inside = jnp.bitwise_and(ids, 127)
    place = jnp.zeros_like(ids)
    for k in range(slot_ref.shape[0]):
        place = jnp.where(block_of == k, slot_ref[k], place)
    columns = (place * BLOCK + inside).astype(jnp.float32)
    beta = beta_ref[...]
    peak = jnp.max(beta, axis=0, keepdims=True)
    total = jnp.sum(jnp.exp(beta - peak), axis=0, keepdims=True)
    msg[...] = jnp.zeros_like(msg)
    msg[0:dpd, :] = columns
    msg[dpd : dpd + 1, :] = peak
    msg[dpd + 1 : dpd + 2, :] = total
    land[me] = msg[...]

    pl.semaphore_wait(barrier, len(peers) + len(mates) + len(others))

    def msg_copy(off, peer, source):
        return send(msg, land.at[source], msg_send.at[off], msg_recv.at[source], {"doc": peer})

    for off, peer in peers:
        msg_copy(off, peer, me).start()

    drift = drift_ref[...]
    var = jnp.full_like(drift, INIT_VAR)
    filt = []
    for k in range(n_tm):
        precision = prec_ref[k : k + 1, :]
        inverse = 1.0 / (1.0 + var * precision)
        gain[k : k + 1, :] = var * precision * inverse
        filt.append(var * inverse)
        var = filt[k] + drift
    info = jnp.zeros_like(drift)
    for k in reversed(range(n_tm)):
        share[k : k + 1, :] = 1.0 / (1.0 + filt[k] * info)
        precision = prec_ref[k : k + 1, :]
        merged = info + precision
        back[k : k + 1, :] = precision / merged
        info = merged / (1.0 + drift * merged)
    cnt = cnt_ref[...].astype(jnp.float32)
    scale = [jnp.transpose(jnp.broadcast_to(cnt[i : i + 1, :], (128, 128))) for i in range(dpd)]
    prior = prior_ref[...]
    alpha = exp_digamma(prior + jnp.sum(cnt, axis=1, keepdims=True) / K)

    for off, peer in peers:
        msg_copy(off, peer, peer).wait_recv()

    peaks = [land[s, dpd : dpd + 1, :] for s in range(n_doc)]
    peak = functools.reduce(jnp.maximum, peaks)
    total = sum(land[s, dpd + 1 : dpd + 2, :] * jnp.exp(peaks[s] - peak) for s in range(n_doc))
    table[...] = (beta_ref[...] - (peak + jnp.log(total))).astype(jnp.bfloat16)

    base = (me * own).astype(jnp.float32)
    lanes = lax.broadcasted_iota(jnp.int32, (128, 128), 1).astype(jnp.float32)

    def row_copy(peer, source):
        return send(rows_out.at[peer], rows_in.at[source], row_send.at[peer], row_recv.at[source], {"doc": peer})

    def look_up(k, _):
        s = lax.rem(me + 3 * (k + 1), n_doc)
        marks = []
        for i in range(dpd):
            col = jnp.transpose(jnp.broadcast_to(land[s, pl.ds(i, 1), :], (128, 128))) - base
            marks.append(
                jnp.concatenate(
                    [(col == lanes + float(128 * j)).astype(jnp.bfloat16) for j in range(own // 128)], axis=1
                )
            )
        looked = jnp.dot(jnp.concatenate(marks, axis=0), table[...], preferred_element_type=jnp.float32)
        rows_out[s] = looked.astype(jnp.bfloat16)

        @pl.when(k < n_doc - 1)
        def _():
            row_copy(s, me).start()

        return 0

    lax.fori_loop(0, n_doc, look_up, 0)
    rows_in[me] = rows_out[me]
    for _, peer in peers:
        row_copy(peer, peer).wait_recv()

    for i in range(dpd):
        at = slice(i * 128, (i + 1) * 128)
        looked = rows_in[0, at, :].astype(jnp.float32)
        for s in range(1, n_doc):
            looked = looked + rows_in[s, at, :].astype(jnp.float32)
        expo[at, :] = jnp.exp(looked - jnp.max(looked, axis=1, keepdims=True))
    for sweep in range(EITERS):
        sums = []
        for i in range(dpd):
            at = slice(i * 128, (i + 1) * 128)
            scaled = expo[at, :] * alpha[i : i + 1, :]
            scaled = scaled * (scale[i] * (1.0 / jnp.sum(scaled, axis=1, keepdims=True)))
            if sweep == EITERS - 1:
                weighted[me, at, :] = scaled.astype(jnp.bfloat16)
            sums.append(jnp.sum(scaled, axis=0, keepdims=True))
        topics = prior + jnp.concatenate(sums, axis=0)
        if sweep < EITERS - 1:
            alpha = exp_digamma(topics)

    def wgt_copy(off, peer, source):
        return send(weighted.at[source], weighted.at[source], wgt_send.at[off], wgt_recv.at[source], {"doc": peer})

    for off, peer in sorted(peers, key=lambda p: abs(p[0] - n_doc // 2)):
        wgt_copy(off, peer, me).start()
    topics_ref[...] = topics

    def tally(s, first, length):
        words = (lax.broadcasted_iota(jnp.int32, (length, 128), 0) + (first + me * own)).astype(jnp.float32)
        marks = jnp.concatenate(
            [(words == land[s, i : i + 1, :]).astype(jnp.bfloat16) for i in range(dpd)], axis=1
        )
        return jnp.dot(marks, weighted[s], preferred_element_type=jnp.float32)

    tile = min(own, 512)

    def first_tally(w, _):
        first = pl.multiple_of(w * tile, tile)
        counts[pl.ds(first, tile), :] = tally(me, first, tile)
        return 0

    lax.fori_loop(0, own // tile, first_tally, 0)
    arrival = sorted(peers, key=lambda p: -abs(p[0] - n_doc // 2))
    for off, peer in arrival[:-1]:
        wgt_copy(off, peer, peer).wait_recv()

        def more_tally(w, _, peer=peer):
            first = pl.multiple_of(w * tile, tile)
            counts[pl.ds(first, tile), :] += tally(peer, first, tile)
            return 0

        lax.fori_loop(0, own // tile, more_tally, 0)
    off, final = arrival[-1]
    wgt_copy(off, final, final).wait_recv()

    def word_rows(mate, c):
        return pl.ds(pl.multiple_of(mate * span + c * width, width), width)

    def in_copy(c, mate, source):
        return send(
            pseudo.at[word_rows(mate, c), :], years_in.at[c, source], in_send.at[c, mate], in_recv.at[c, source], mate_id(mate)
        )

    def last_tally(k, _):
        c = k // GROUP
        mate = lax.rem(m + 1 + lax.rem(k, GROUP), GROUP)
        at = word_rows(mate, c)
        whole = counts[at, :] + tally(final, mate * span + c * width, width)
        pseudo[at, :] = beta_ref[at, :] + jnp.log1p(whole)

        @pl.when(mate != m)
        def _():
            in_copy(c, mate, m).start()

        return 0

    lax.fori_loop(0, CHUNKS * GROUP, last_tally, 0)

    first_year = b * GROUP
    g = [gain[pl.ds(first_year + i, 1), :] for i in range(GROUP)]
    r = [back[pl.ds(first_year + i, 1), :] for i in range(GROUP)]
    w = [share[pl.ds(first_year + i, 1), :] for i in range(GROUP)]
    keep = []
    for i in range(GROUP):
        keep.append((1.0 - g[i]) * keep[-1] if i else 1.0 - g[i])
    hold = [jnp.ones_like(g[0])]
    for i in reversed(range(GROUP)):
        hold.insert(0, (1.0 - r[i]) * hold[0])
    block_keep, block_hold = [], []
    for other in range(n_blocks):
        years = range(other * GROUP, (other + 1) * GROUP)
        block_keep.append(functools.reduce(jnp.multiply, [1.0 - gain[y : y + 1, :] for y in years]))
        block_hold.append(functools.reduce(jnp.multiply, [1.0 - back[y : y + 1, :] for y in years]))
    into = []
    for other in range(n_blocks):
        fore = jnp.where(other < b, 1.0, 0.0)
        for between in range(other + 1, n_blocks):
            fore = fore * jnp.where(between < b, block_keep[between], 1.0)
        hind = jnp.where(other > b, 1.0, 0.0)
        for between in range(other):
            hind = hind * jnp.where(between > b, block_hold[between], 1.0)
        into.append((fore, hind))

    def mid_copy(c, off, other, source):
        which = jnp.where(other > b, 0, 1)
        return send(mid_out.at[c, which], mid_in.at[c, source], mid_send.at[c, off], mid_recv.at[c, source], other_id(other))

    for c in range(CHUNKS):
        years_in[c, m] = pseudo[word_rows(m, c), :]
        mid_in[c, b] = jnp.zeros((width, K), jnp.float32)
        for off, mate in mates:
            in_copy(c, mate, mate).wait_recv()
        ahead = g[0] * years_in[c, 0]
        local[c, 0] = w[0] * ahead
        for i in range(1, GROUP):
            ahead = g[i] * years_in[c, i] + (1.0 - g[i]) * ahead
            local[c, i] = w[i] * ahead
        mid_out[c, 0] = ahead
        behind = r[GROUP - 1] * years_in[c, GROUP - 1]
        for i in reversed(range(GROUP - 1)):
            local[c, i] += (1.0 - w[i]) * behind
            behind = r[i] * years_in[c, i] + (1.0 - r[i]) * behind
        mid_out[c, 1] = behind
        for off, other in others:
            mid_copy(c, off, other, b).start()

    def out_copy(c, mate, source):
        return send(
            years_out.at[c, mate], out_ref.at[word_rows(source, c), :], out_send.at[c, mate], out_recv.at[c, source], mate_id(mate)
        )

    for c in range(CHUNKS):
        for off, other in others:
            mid_copy(c, off, other, other).wait_recv()
        ahead, behind = 0.0, 0.0
        for other in range(n_blocks):
            value = mid_in[c, other]
            ahead = ahead + into[other][0] * value
            behind = behind + into[other][1] * value
        for i in range(GROUP):
            years_out[c, i] = local[c, i] + (w[i] * keep[i]) * ahead + ((1.0 - w[i]) * hold[i + 1]) * behind
        for off, mate in mates:
            out_copy(c, mate, m).start()
        out_ref[word_rows(m, c), :] = years_out[c, m]

    for c in range(CHUNKS):
        for off, mate in mates:
            out_copy(c, mate, mate).wait_recv()
    for off, peer in peers:
        msg_copy(off, peer, me).wait_send()
        row_copy(peer, me).wait_send()
        wgt_copy(off, peer, me).wait_send()
    for c in range(CHUNKS):
        for off, mate in mates:
            in_copy(c, mate, m).wait_send()
            out_copy(c, mate, m).wait_send()
        for off, other in others:
            mid_copy(c, off, other, b).wait_send()


def vmem():
    return pl.BlockSpec(memory_space=pltpu.VMEM)


def solution(mesh):
    n_tm, n_doc = mesh.shape["tm"], mesh.shape["doc"]

    def body(beta, word_ids, word_counts, block_slot, topic_prior, drift_var, obs_precision):
        local_beta, ids, cnt = beta[0], word_ids[0], word_counts[0]
        own, dpd = local_beta.shape[0], ids.shape[0]
        held = dpd * 128
        width = own // GROUP // CHUNKS
        n_blocks = n_tm // GROUP
        f32, bf16 = jnp.float32, jnp.bfloat16
        dma = pltpu.SemaphoreType.DMA
        smoothed, doc_topics = pl.pallas_call(
            functools.partial(kernel, n_tm, n_doc),
            out_shape=(jax.ShapeDtypeStruct((own, K), f32), jax.ShapeDtypeStruct((dpd, K), f32)),
            in_specs=[vmem(), vmem(), vmem(), pl.BlockSpec(memory_space=pltpu.SMEM), vmem(), vmem(), vmem()],
            out_specs=(vmem(), vmem()),
            scratch_shapes=[
                pltpu.VMEM((8, K), f32),
                pltpu.VMEM((n_doc, 8, K), f32),
                pltpu.VMEM((own, K), bf16),
                pltpu.VMEM((n_doc, held, K), bf16),
                pltpu.VMEM((n_doc, held, K), bf16),
                pltpu.VMEM((held, K), f32),
                pltpu.VMEM((n_doc, held, K), bf16),
                pltpu.VMEM((own, K), f32),
                pltpu.VMEM((n_tm, K), f32),
                pltpu.VMEM((n_tm, K), f32),
                pltpu.VMEM((n_tm, K), f32),
                pltpu.VMEM((own, K), f32),
                pltpu.VMEM((CHUNKS, GROUP, width, K), f32),
                pltpu.VMEM((CHUNKS, GROUP, width, K), f32),
                pltpu.VMEM((CHUNKS, 2, width, K), f32),
                pltpu.VMEM((CHUNKS, n_blocks, width, K), f32),
                pltpu.VMEM((CHUNKS, GROUP, width, K), f32),
                dma((n_doc,)),
                dma((n_doc,)),
                dma((n_doc,)),
                dma((n_doc,)),
                dma((n_doc,)),
                dma((n_doc,)),
                dma((CHUNKS, GROUP)),
                dma((CHUNKS, GROUP)),
                dma((CHUNKS, n_blocks)),
                dma((CHUNKS, n_blocks)),
                dma((CHUNKS, GROUP)),
                dma((CHUNKS, GROUP)),
            ],
            compiler_params=pltpu.CompilerParams(
                collective_id=0, has_side_effects=True, vmem_limit_bytes=48 * 1024 * 1024
            ),
            name="topics",
        )(local_beta, ids, cnt, block_slot, topic_prior[None], obs_precision, drift_var[None])
        return (smoothed[None], doc_topics[None])

    in_specs = (P("tm", "doc", None), P("tm", "doc", None), P("tm", "doc", None), P(), P(), P(), P())
    out_specs = (P("tm", "doc", None), P("tm", "doc", None))
    return jax.shard_map(body, mesh=mesh, in_specs=in_specs, out_specs=out_specs, check_vma=False)
```

time: 717 us -> 92 us (0.13)
  the two profiles are of different devices: /device:TPU:1 before, /device:TPU:7 now
where the time goes in v2:
time: 92 us; the launch traced here: 91.8 us
  Pallas kernels  86.9 us (94%)
  local copies, waits for them, and re-layouts  4.17 us (5%)
    pallas_call x1, Pallas kernels, body(): pl.pallas_call(functools.partial(kernel, n_tm, n_doc), out_shape=(jax.Sha...  86.9 us
    unnamed x16, local copies, waits for them, and re-layouts  4.17 us

profile of v2, /device:TPU:7, one launch (start us, length us, event | category | flops | bytes accessed | tf_op | source)
XLA Modules:
  0.0 91.8 jit_solution(4771219706602585827)
XLA Ops:
  0.6 0.0 copy-start.3
  0.6 0.0 copy-start.2
  0.7 0.0 copy-start.4
  0.7 0.0 copy-start.5
  0.7 0.0 copy-start.6
  0.7 0.6 copy-done.3
  1.3 0.0 copy-done.2
  1.3 0.0 copy-done.4
  1.3 0.0 copy-done.5
  1.3 0.0 copy-done.6
  1.4 0.0 copy-start
  1.4 1.2 %copy-done = f32[1,2048,128]{2,1,0:T(8,128)S(1)} copy-done((f32[1,2048,128]{2,1,0:T(8,128)S(1)}, f32[1,2048,128]{2,1,0:T(8,128)}, u32[]{:S(2)}) %copy-start) | copy-done | bytes 1048600
  2.6 0.0 copy-start.1
  2.6 0.7 copy-done.1
  3.3 86.9 %topics.1 = (f32[2048,128]{1,0:T(8,128)S(1)}, f32[4,128]{1,0:T(4,128)S(1)}) custom-call(f32[2048,128]{1,0:T(8,128)S(1)} %bitcast.7, s32[4,128]{1,0:T(4,128)S(1)} %bitcast.9, s32[4,128]{1,0:T(4,128)S(1)} %bitcast.10, s32[128]{0:T(128)S(1)} %copy-done.4, f32[1,128]{1,0:T(1,128)S(1)} %bitcast.12, f32[32,128]{1,0:T(8,128)S(1)} %copy-done.1, f32[1,128]{1,0:T(1,128)S(1)} %bitcast.13), custom_call_target="tpu_custom_call" | custom-call | tf_op jit(solution)/shard_map/topics/pallas_call | solution.py:363
  90.3 1.0 %copy.11 = f32[1,2048,128]{2,1,0:T(8,128)} copy(f32[1,2048,128]{2,1,0:T(8,128)S(1)} %bitcast.8) | data formatting | bytes 2097152
  91.2 0.6 copy.12
Async XLA Ops:
  0.6 0.7 copy-start.3
  0.6 0.7 copy-start.2
  0.7 0.7 copy-start.4
  0.7 0.7 copy-start.5
  0.7 0.7 copy-start.6
  1.4 1.2 %copy-start = (f32[1,2048,128]{2,1,0:T(8,128)S(1)}, f32[1,2048,128]{2,1,0:T(8,128)}, u32[]{:S(2)}) copy-start(f32[1,2048,128]{2,1,0:T(8,128)} %param.7) | copy-start | bytes 3145732
  2.6 0.7 copy-start.1

commit v3 on v2

--- a/solution.py
+++ b/solution.py
@@ -11,6 +11,7 @@
 BLOCK = 128
 EITERS = 4
 GROUP = 8
+FOLD = 4
 CHUNKS = 2
 INIT_VAR = 4.0
 MESH = pl.DeviceIdType.MESH
@@ -47,11 +48,15 @@
     msg,
     land,
     table,
-    rows_out,
-    rows_in,
     expo,
+    scale,
+    quarter,
     weighted,
-    counts,
+    alpha,
+    part,
+    sums,
+    end_part,
+    end_sums,
     gain,
     back,
     share,
@@ -63,10 +68,10 @@
     years_out,
     msg_send,
     msg_recv,
-    row_send,
-    row_recv,
-    wgt_send,
-    wgt_recv,
+    sum_send,
+    sum_recv,
+    end_send,
+    end_recv,
     in_send,
     in_recv,
     mid_send,
@@ -117,6 +122,7 @@
     msg[0:dpd, :] = columns
     msg[dpd : dpd + 1, :] = peak
     msg[dpd + 1 : dpd + 2, :] = total
+    msg[8 : 8 + dpd, :] = cnt_ref[...].astype(jnp.float32)
     land[me] = msg[...]
 
     pl.semaphore_wait(barrier, len(peers) + len(mates) + len(others))
@@ -143,10 +149,7 @@
         merged = info + precision
         back[k : k + 1, :] = precision / merged
         info = merged / (1.0 + drift * merged)
-    cnt = cnt_ref[...].astype(jnp.float32)
-    scale = [jnp.transpose(jnp.broadcast_to(cnt[i : i + 1, :], (128, 128))) for i in range(dpd)]
     prior = prior_ref[...]
-    alpha = exp_digamma(prior + jnp.sum(cnt, axis=1, keepdims=True) / K)
 
     for off, peer in peers:
         msg_copy(off, peer, peer).wait_recv()
@@ -154,91 +157,89 @@
     peaks = [land[s, dpd : dpd + 1, :] for s in range(n_doc)]
     peak = functools.reduce(jnp.maximum, peaks)
     total = sum(land[s, dpd + 1 : dpd + 2, :] * jnp.exp(peaks[s] - peak) for s in range(n_doc))
-    table[...] = (beta_ref[...] - (peak + jnp.log(total))).astype(jnp.bfloat16)
+    normalizer = peak + jnp.log(total)
+    fold = own // FOLD
+    for f in range(FOLD):
+        table[:, f * K : (f + 1) * K] = (beta_ref[f * fold : (f + 1) * fold, :] - normalizer).astype(jnp.bfloat16)
 
     base = (me * own).astype(jnp.float32)
     lanes = lax.broadcasted_iota(jnp.int32, (128, 128), 1).astype(jnp.float32)
 
-    def row_copy(peer, source):
-        return send(rows_out.at[peer], rows_in.at[source], row_send.at[peer], row_recv.at[source], {"doc": peer})
-
-    def look_up(k, _):
-        s = lax.rem(me + 3 * (k + 1), n_doc)
-        marks = []
+    for s in range(n_doc):
+        start = jnp.sum(land[s, 8 : 8 + dpd, :], axis=1, keepdims=True) / K
+        alpha[s * dpd : (s + 1) * dpd, :] = jnp.broadcast_to(start, (dpd, K))
+    alpha[...] = exp_digamma(prior + alpha[...])
+
+    def look_up(s, _):
+        marks, parts = [], []
         for i in range(dpd):
-            col = jnp.transpose(jnp.broadcast_to(land[s, pl.ds(i, 1), :], (128, 128))) - base
+            both = land[s, pl.ds(i, 1), :] * 16.0 + land[s, pl.ds(8 + i, 1), :]
+            both = jnp.transpose(jnp.broadcast_to(both, (128, 128)))
+            col = jnp.floor(both * (1.0 / 16.0))
+            cnt = both - 16.0 * col
+            col = col - base
+            part_of = jnp.floor(col * (1.0 / fold))
+            rest = col - float(fold) * part_of
+            parts.append(part_of)
+            at = pl.ds(pl.multiple_of((s * dpd + i) * 128, 128), 128)
+            scale[at, :] = jnp.where((part_of >= 0.0) & (part_of < float(FOLD)), cnt, 0.0)
+            quarter[at, :] = part_of
             marks.append(
                 jnp.concatenate(
-                    [(col == lanes + float(128 * j)).astype(jnp.bfloat16) for j in range(own // 128)], axis=1
+                    [(rest == lanes + float(128 * j)).astype(jnp.bfloat16) for j in range(fold // 128)], axis=1
                 )
             )
-        looked = jnp.dot(jnp.concatenate(marks, axis=0), table[...], preferred_element_type=jnp.float32)
-        rows_out[s] = looked.astype(jnp.bfloat16)
-
-        @pl.when(k < n_doc - 1)
-        def _():
-            row_copy(s, me).start()
-
+        wide = jnp.dot(jnp.concatenate(marks, axis=0), table[...], preferred_element_type=jnp.float32)
+        part_of = jnp.concatenate(parts, axis=0)
+        looked = wide[:, 0:K]
+        for f in range(1, FOLD):
+            looked = jnp.where(part_of == float(f), wide[:, f * K : (f + 1) * K], looked)
+        at = pl.ds(pl.multiple_of(s * held, held), held)
+        expo[at, :] = jnp.exp(looked - jnp.max(looked, axis=1, keepdims=True))
         return 0
 
     lax.fori_loop(0, n_doc, look_up, 0)
-    rows_in[me] = rows_out[me]
-    for _, peer in peers:
-        row_copy(peer, peer).wait_recv()
-
-    for i in range(dpd):
-        at = slice(i * 128, (i + 1) * 128)
-        looked = rows_in[0, at, :].astype(jnp.float32)
-        for s in range(1, n_doc):
-            looked = looked + rows_in[s, at, :].astype(jnp.float32)
-        expo[at, :] = jnp.exp(looked - jnp.max(looked, axis=1, keepdims=True))
+
+    def sum_copy(sweep, off, peer, source):
+        return send(part.at[sweep], sums.at[sweep, source], sum_send.at[sweep, off], sum_recv.at[sweep, source], {"doc": peer})
+
+    def end_copy(off, peer, source):
+        return send(end_part.at[peer], end_sums.at[source], end_send.at[off], end_recv.at[source], {"doc": peer})
+
     for sweep in range(EITERS):
-        sums = []
-        for i in range(dpd):
-            at = slice(i * 128, (i + 1) * 128)
-            scaled = expo[at, :] * alpha[i : i + 1, :]
-            scaled = scaled * (scale[i] * (1.0 / jnp.sum(scaled, axis=1, keepdims=True)))
-            if sweep == EITERS - 1:
-                weighted[me, at, :] = scaled.astype(jnp.bfloat16)
-            sums.append(jnp.sum(scaled, axis=0, keepdims=True))
-        topics = prior + jnp.concatenate(sums, axis=0)
-        if sweep < EITERS - 1:
-            alpha = exp_digamma(topics)
-
-    def wgt_copy(off, peer, source):
-        return send(weighted.at[source], weighted.at[source], wgt_send.at[off], wgt_recv.at[source], {"doc": peer})
-
-    for off, peer in sorted(peers, key=lambda p: abs(p[0] - n_doc // 2)):
-        wgt_copy(off, peer, me).start()
-    topics_ref[...] = topics
-
-    def tally(s, first, length):
-        words = (lax.broadcasted_iota(jnp.int32, (length, 128), 0) + (first + me * own)).astype(jnp.float32)
-        marks = jnp.concatenate(
-            [(words == land[s, i : i + 1, :]).astype(jnp.bfloat16) for i in range(dpd)], axis=1
-        )
-        return jnp.dot(marks, weighted[s], preferred_element_type=jnp.float32)
-
-    tile = min(own, 512)
-
-    def first_tally(w, _):
-        first = pl.multiple_of(w * tile, tile)
-        counts[pl.ds(first, tile), :] = tally(me, first, tile)
-        return 0
-
-    lax.fori_loop(0, own // tile, first_tally, 0)
-    arrival = sorted(peers, key=lambda p: -abs(p[0] - n_doc // 2))
-    for off, peer in arrival[:-1]:
-        wgt_copy(off, peer, peer).wait_recv()
-
-        def more_tally(w, _, peer=peer):
-            first = pl.multiple_of(w * tile, tile)
-            counts[pl.ds(first, tile), :] += tally(peer, first, tile)
+        last = sweep == EITERS - 1
+
+        def e_step(s, _, last=last, sweep=sweep):
+            for i in range(dpd):
+                row = s * dpd + i
+                at = pl.ds(pl.multiple_of(row * 128, 128), 128)
+                scaled = expo[at, :] * alpha[pl.ds(row, 1), :]
+                scaled = scaled * (scale[at, :] * (1.0 / jnp.sum(scaled, axis=1, keepdims=True)))
+                if last:
+                    end_part[s, i : i + 1, :] = jnp.sum(scaled, axis=0, keepdims=True)
+                    for f in range(FOLD):
+                        weighted[at, f * K : (f + 1) * K] = jnp.where(quarter[at, :] == float(f), scaled, 0.0).astype(
+                            jnp.bfloat16
+                        )
+                else:
+                    part[sweep, pl.ds(row, 1), :] = jnp.sum(scaled, axis=0, keepdims=True)
             return 0
 
-        lax.fori_loop(0, own // tile, more_tally, 0)
-    off, final = arrival[-1]
-    wgt_copy(off, final, final).wait_recv()
+        lax.fori_loop(0, n_doc, e_step, 0)
+        if not last:
+            for off, peer in peers:
+                sum_copy(sweep, off, peer, me).start()
+            sums[sweep, me] = part[sweep]
+            for off, peer in peers:
+                sum_copy(sweep, off, peer, peer).wait_recv()
+            whole = sums[sweep, 0]
+            for s in range(1, n_doc):
+                whole = whole + sums[sweep, s]
+            alpha[...] = exp_digamma(prior + whole)
+        else:
+            for off, peer in peers:
+                end_copy(off, peer, me).start()
+            end_sums[me] = end_part[me]
 
     def word_rows(mate, c):
         return pl.ds(pl.multiple_of(mate * span + c * width, width), width)
@@ -248,20 +249,43 @@
             pseudo.at[word_rows(mate, c), :], years_in.at[c, source], in_send.at[c, mate], in_recv.at[c, source], mate_id(mate)
         )
 
-    def last_tally(k, _):
-        c = k // GROUP
-        mate = lax.rem(m + 1 + lax.rem(k, GROUP), GROUP)
-        at = word_rows(mate, c)
-        whole = counts[at, :] + tally(final, mate * span + c * width, width)
-        pseudo[at, :] = beta_ref[at, :] + jnp.log1p(whole)
-
-        @pl.when(mate != m)
-        def _():
-            in_copy(c, mate, m).start()
-
-        return 0
-
-    lax.fori_loop(0, CHUNKS * GROUP, last_tally, 0)
+    spans = fold // span
+    rests = []
+    for s in range(n_doc):
+        col = land[s, 0:dpd, :] - base
+        rests.append(col - float(fold) * jnp.floor(col * (1.0 / fold)))
+    words = lax.broadcasted_iota(jnp.int32, (width, 128), 0).astype(jnp.float32)
+    for c in range(CHUNKS):
+        marks = []
+        for s in range(n_doc):
+            for i in range(dpd):
+                marks.append(
+                    jnp.concatenate(
+                        [
+                            (words + float(h * span + c * width) == rests[s][i : i + 1, :]).astype(jnp.bfloat16)
+                            for h in range(spans)
+                        ],
+                        axis=0,
+                    )
+                )
+        counts = jnp.dot(jnp.concatenate(marks, axis=1), weighted[...], preferred_element_type=jnp.float32)
+        for h in range(spans):
+            for f in range(FOLD):
+                mate = f * spans + h
+                first = mate * span + c * width
+                whole = counts[h * width : (h + 1) * width, f * K : (f + 1) * K]
+                pseudo[first : first + width, :] = beta_ref[first : first + width, :] + jnp.log1p(whole)
+
+                @pl.when(mate != m)
+                def _(mate=mate, c=c):
+                    in_copy(c, mate, m).start()
+
+    for off, peer in peers:
+        end_copy(off, peer, peer).wait_recv()
+    whole = end_sums[0]
+    for s in range(1, n_doc):
+        whole = whole + end_sums[s]
+    topics_ref[...] = prior + whole
 
     first_year = b * GROUP
     g = [gain[pl.ds(first_year + i, 1), :] for i in range(GROUP)]
@@ -335,8 +359,9 @@
             out_copy(c, mate, mate).wait_recv()
     for off, peer in peers:
         msg_copy(off, peer, me).wait_send()
-        row_copy(peer, me).wait_send()
-        wgt_copy(off, peer, me).wait_send()
+        for sweep in range(EITERS - 1):
+            sum_copy(sweep, off, peer, me).wait_send()
+        end_copy(off, peer, me).wait_send()
     for c in range(CHUNKS):
         for off, mate in mates:
             in_copy(c, mate, m).wait_send()
@@ -366,14 +391,18 @@
             in_specs=[vmem(), vmem(), vmem(), pl.BlockSpec(memory_space=pltpu.SMEM), vmem(), vmem(), vmem()],
             out_specs=(vmem(), vmem()),
             scratch_shapes=[
-                pltpu.VMEM((8, K), f32),
-                pltpu.VMEM((n_doc, 8, K), f32),
-                pltpu.VMEM((own, K), bf16),
-                pltpu.VMEM((n_doc, held, K), bf16),
-                pltpu.VMEM((n_doc, held, K), bf16),
-                pltpu.VMEM((held, K), f32),
-                pltpu.VMEM((n_doc, held, K), bf16),
-                pltpu.VMEM((own, K), f32),
+                pltpu.VMEM((16, K), f32),
+                pltpu.VMEM((n_doc, 16, K), f32),
+                pltpu.VMEM((own // FOLD, FOLD * K), bf16),
+                pltpu.VMEM((n_doc * held, K), f32),
+                pltpu.VMEM((n_doc * held, K), f32),
+                pltpu.VMEM((n_doc * held, K), f32),
+                pltpu.VMEM((n_doc * held, FOLD * K), bf16),
+                pltpu.VMEM((n_doc * dpd, K), f32),
+                pltpu.VMEM((EITERS - 1, n_doc * dpd, K), f32),
+                pltpu.VMEM((EITERS - 1, n_doc, n_doc * dpd, K), f32),
+                pltpu.VMEM((n_doc, dpd, K), f32),
+                pltpu.VMEM((n_doc, dpd, K), f32),
                 pltpu.VMEM((n_tm, K), f32),
                 pltpu.VMEM((n_tm, K), f32),
                 pltpu.VMEM((n_tm, K), f32),
@@ -385,8 +414,8 @@
                 pltpu.VMEM((CHUNKS, GROUP, width, K), f32),
                 dma((n_doc,)),
                 dma((n_doc,)),
-                dma((n_doc,)),
-                dma((n_doc,)),
+                dma((EITERS - 1, n_doc)),
+                dma((EITERS - 1, n_doc)),
                 dma((n_doc,)),
                 dma((n_doc,)),
                 dma((CHUNKS, GROUP)),

time: 92 us -> 79.8 us (0.87)
  the two profiles are of different devices: /device:TPU:7 before, /device:TPU:1 now
where the time goes in v3:
time: 79.8 us; the launch traced here: 79 us
  Pallas kernels  74.2 us (93%)
  local copies, waits for them, and re-layouts  4.17 us (5%)
    pallas_call x1, Pallas kernels, body(): pl.pallas_call(functools.partial(kernel, n_tm, n_doc), out_shape=(jax.Sha...  74.2 us
    unnamed x16, local copies, waits for them, and re-layouts  4.17 us

profile of v3, /device:TPU:1, one launch (start us, length us, event | category | flops | bytes accessed | tf_op | source)
XLA Modules:
  0.0 79.0 jit_solution(11686518532160156891)
XLA Ops:
  0.6 0.0 copy-start.3
  0.6 0.0 copy-start.2
  0.7 0.0 copy-start.4
  0.7 0.0 copy-start.5
  0.7 0.0 copy-start.6
  0.7 0.6 copy-done.3
  1.3 0.0 copy-done.2
  1.3 0.0 copy-done.4
  1.3 0.0 copy-done.5
  1.3 0.0 copy-done.6
  1.4 0.0 copy-start
  1.4 1.2 %copy-done = f32[1,2048,128]{2,1,0:T(8,128)S(1)} copy-done((f32[1,2048,128]{2,1,0:T(8,128)S(1)}, f32[1,2048,128]{2,1,0:T(8,128)}, u32[]{:S(2)}) %copy-start) | copy-done | bytes 1048600
  2.6 0.0 copy-start.1
  2.6 0.7 copy-done.1
  3.3 74.2 %topics.1 = (f32[2048,128]{1,0:T(8,128)S(1)}, f32[4,128]{1,0:T(4,128)S(1)}) custom-call(f32[2048,128]{1,0:T(8,128)S(1)} %bitcast.7, s32[4,128]{1,0:T(4,128)S(1)} %bitcast.9, s32[4,128]{1,0:T(4,128)S(1)} %bitcast.10, s32[128]{0:T(128)S(1)} %copy-done.4, f32[1,128]{1,0:T(1,128)S(1)} %bitcast.12, f32[32,128]{1,0:T(8,128)S(1)} %copy-done.1, f32[1,128]{1,0:T(1,128)S(1)} %bitcast.13), custom_call_target="tpu_custom_call" | custom-call | tf_op jit(solution)/shard_map/topics/pallas_call | solution.py:388
  77.5 1.0 %copy.11 = f32[1,2048,128]{2,1,0:T(8,128)} copy(f32[1,2048,128]{2,1,0:T(8,128)S(1)} %bitcast.8) | data formatting | bytes 2097152
  78.5 0.6 copy.12
Async XLA Ops:
  0.6 0.7 copy-start.3
  0.6 0.7 copy-start.2
  0.7 0.7 copy-start.4
  0.7 0.7 copy-start.5
  0.7 0.7 copy-start.6
  1.4 1.2 %copy-start = (f32[1,2048,128]{2,1,0:T(8,128)S(1)}, f32[1,2048,128]{2,1,0:T(8,128)}, u32[]{:S(2)}) copy-start(f32[1,2048,128]{2,1,0:T(8,128)} %param.7) | copy-start | bytes 3145732
  2.6 0.7 copy-start.1

commit v4 on v3

--- a/solution.py
+++ b/solution.py
@@ -1,4 +1,5 @@
 import functools
+import math
 
 import jax
 import jax.numpy as jnp
@@ -27,15 +28,45 @@
     return y * jnp.exp(-(series + steps))
 
 
+FLOOR = 2.0**-10
+LIMIT = 300.0
+STEPS = 32766.0 / math.log2(1.0 + LIMIT / FLOOR)
+
+
+def encode(value):
+    size = jnp.log2(1.0 + jnp.abs(value) * (1.0 / FLOOR)) * STEPS + 0.5
+    code = size.astype(jnp.int32)
+    return jnp.where(value < 0.0, -code, code).astype(jnp.int16)
+
+
+def decode(code):
+    code = code.astype(jnp.float32)
+    size = jnp.exp2(jnp.abs(code) * (1.0 / STEPS)) * FLOOR - FLOOR
+    return jnp.where(code < 0.0, -size, size)
+
+
 def send(src, dst, send_sem, recv_sem, where):
     return pltpu.make_async_remote_copy(
         src_ref=src, dst_ref=dst, send_sem=send_sem, recv_sem=recv_sem, device_id=where, device_id_type=MESH
     )
 
 
+def far_first(count):
+    return sorted(range(1, count), key=lambda off: abs(off - count // 2) + 2 * (1 - off % 2))
+
+
 def kernel(
     n_tm,
     n_doc,
+    beta_hbm,
+    ids_hbm,
+    cnt_hbm,
+    slot_hbm,
+    prior_hbm,
+    prec_hbm,
+    drift_hbm,
+    out_ref,
+    topics_ref,
     beta_ref,
     ids_ref,
     cnt_ref,
@@ -43,8 +74,7 @@
     prior_ref,
     prec_ref,
     drift_ref,
-    out_ref,
-    topics_ref,
+    load_sem,
     msg,
     land,
     table,
@@ -66,6 +96,7 @@
     mid_out,
     mid_in,
     years_out,
+    coded,
     msg_send,
     msg_recv,
     sum_send,
@@ -90,7 +121,7 @@
     span = own // GROUP
     width = span // CHUNKS
 
-    peers = [(off, lax.rem(me + off, n_doc)) for off in range(1, n_doc)]
+    peers = [(off, lax.rem(me + off, n_doc)) for off in far_first(n_doc)]
     mates = [(off, lax.rem(m + off, GROUP)) for off in range(1, GROUP)]
     others = [(off, lax.rem(b + off, n_blocks)) for off in range(1, n_blocks)]
 
@@ -107,6 +138,25 @@
         pl.semaphore_signal(barrier, inc=1, device_id=mate_id(mate), device_id_type=MESH)
     for _, other in others:
         pl.semaphore_signal(barrier, inc=1, device_id=other_id(other), device_id_type=MESH)
+
+    loads = [
+        pltpu.make_async_copy(source, held_here, load_sem.at[k])
+        for k, (source, held_here) in enumerate(
+            [
+                (ids_hbm, ids_ref),
+                (slot_hbm, slot_ref),
+                (cnt_hbm, cnt_ref),
+                (beta_hbm, beta_ref),
+                (prec_hbm, prec_ref),
+                (drift_hbm, drift_ref),
+                (prior_hbm, prior_ref),
+            ]
+        )
+    ]
+    for load in loads:
+        load.start()
+    for load in loads:
+        load.wait()
 
     ids = ids_ref[...]
     block_of = lax.shift_right_logical(ids, 7)
@@ -198,7 +248,7 @@
         expo[at, :] = jnp.exp(looked - jnp.max(looked, axis=1, keepdims=True))
         return 0
 
-    lax.fori_loop(0, n_doc, look_up, 0)
+    lax.fori_loop(0, n_doc, look_up, 0, unroll=2)
 
     def sum_copy(sweep, off, peer, source):
         return send(part.at[sweep], sums.at[sweep, source], sum_send.at[sweep, off], sum_recv.at[sweep, source], {"doc": peer})
@@ -225,7 +275,7 @@
                     part[sweep, pl.ds(row, 1), :] = jnp.sum(scaled, axis=0, keepdims=True)
             return 0
 
-        lax.fori_loop(0, n_doc, e_step, 0)
+        lax.fori_loop(0, n_doc, e_step, 0, unroll=2)
         if not last:
             for off, peer in peers:
                 sum_copy(sweep, off, peer, me).start()
@@ -274,7 +324,7 @@
                 mate = f * spans + h
                 first = mate * span + c * width
                 whole = counts[h * width : (h + 1) * width, f * K : (f + 1) * K]
-                pseudo[first : first + width, :] = beta_ref[first : first + width, :] + jnp.log1p(whole)
+                pseudo[first : first + width, :] = encode(beta_ref[first : first + width, :] + jnp.log1p(whole))
 
                 @pl.when(mate != m)
                 def _(mate=mate, c=c):
@@ -318,26 +368,27 @@
 
     for c in range(CHUNKS):
         years_in[c, m] = pseudo[word_rows(m, c), :]
-        mid_in[c, b] = jnp.zeros((width, K), jnp.float32)
+        mid_in[c, b] = jnp.zeros((width, K), jnp.int16)
         for off, mate in mates:
             in_copy(c, mate, mate).wait_recv()
-        ahead = g[0] * years_in[c, 0]
+        values = [decode(years_in[c, i]) for i in range(GROUP)]
+        ahead = g[0] * values[0]
         local[c, 0] = w[0] * ahead
         for i in range(1, GROUP):
-            ahead = g[i] * years_in[c, i] + (1.0 - g[i]) * ahead
+            ahead = g[i] * values[i] + (1.0 - g[i]) * ahead
             local[c, i] = w[i] * ahead
-        mid_out[c, 0] = ahead
-        behind = r[GROUP - 1] * years_in[c, GROUP - 1]
+        mid_out[c, 0] = encode(ahead)
+        behind = r[GROUP - 1] * values[GROUP - 1]
         for i in reversed(range(GROUP - 1)):
             local[c, i] += (1.0 - w[i]) * behind
-            behind = r[i] * years_in[c, i] + (1.0 - r[i]) * behind
-        mid_out[c, 1] = behind
+            behind = r[i] * values[i] + (1.0 - r[i]) * behind
+        mid_out[c, 1] = encode(behind)
         for off, other in others:
             mid_copy(c, off, other, b).start()
 
     def out_copy(c, mate, source):
         return send(
-            years_out.at[c, mate], out_ref.at[word_rows(source, c), :], out_send.at[c, mate], out_recv.at[c, source], mate_id(mate)
+            years_out.at[c, mate], coded.at[word_rows(source, c), :], out_send.at[c, mate], out_recv.at[c, source], mate_id(mate)
         )
 
     for c in range(CHUNKS):
@@ -345,18 +396,19 @@
             mid_copy(c, off, other, other).wait_recv()
         ahead, behind = 0.0, 0.0
         for other in range(n_blocks):
-            value = mid_in[c, other]
+            value = decode(mid_in[c, other])
             ahead = ahead + into[other][0] * value
             behind = behind + into[other][1] * value
         for i in range(GROUP):
-            years_out[c, i] = local[c, i] + (w[i] * keep[i]) * ahead + ((1.0 - w[i]) * hold[i + 1]) * behind
+            years_out[c, i] = encode(local[c, i] + (w[i] * keep[i]) * ahead + ((1.0 - w[i]) * hold[i + 1]) * behind)
         for off, mate in mates:
             out_copy(c, mate, m).start()
-        out_ref[word_rows(m, c), :] = years_out[c, m]
+        out_ref[word_rows(m, c), :] = decode(years_out[c, m])
 
     for c in range(CHUNKS):
         for off, mate in mates:
             out_copy(c, mate, mate).wait_recv()
+            out_ref[word_rows(mate, c), :] = decode(coded[word_rows(mate, c), :])
     for off, peer in peers:
         msg_copy(off, peer, me).wait_send()
         for sweep in range(EITERS - 1):
@@ -383,14 +435,22 @@
         held = dpd * 128
         width = own // GROUP // CHUNKS
         n_blocks = n_tm // GROUP
-        f32, bf16 = jnp.float32, jnp.bfloat16
+        f32, bf16, link = jnp.float32, jnp.bfloat16, jnp.int16
         dma = pltpu.SemaphoreType.DMA
         smoothed, doc_topics = pl.pallas_call(
             functools.partial(kernel, n_tm, n_doc),
             out_shape=(jax.ShapeDtypeStruct((own, K), f32), jax.ShapeDtypeStruct((dpd, K), f32)),
-            in_specs=[vmem(), vmem(), vmem(), pl.BlockSpec(memory_space=pltpu.SMEM), vmem(), vmem(), vmem()],
+            in_specs=[pl.BlockSpec(memory_space=pltpu.HBM)] * 7,
             out_specs=(vmem(), vmem()),
             scratch_shapes=[
+                pltpu.VMEM((own, K), f32),
+                pltpu.VMEM((dpd, 128), jnp.int32),
+                pltpu.VMEM((dpd, 128), jnp.int32),
+                pltpu.SMEM(block_slot.shape, jnp.int32),
+                pltpu.VMEM((1, K), f32),
+                pltpu.VMEM((n_tm, K), f32),
+                pltpu.VMEM((1, K), f32),
+                dma((7,)),
                 pltpu.VMEM((16, K), f32),
                 pltpu.VMEM((n_doc, 16, K), f32),
                 pltpu.VMEM((own // FOLD, FOLD * K), bf16),
@@ -406,12 +466,13 @@
                 pltpu.VMEM((n_tm, K), f32),
                 pltpu.VMEM((n_tm, K), f32),
                 pltpu.VMEM((n_tm, K), f32),
-                pltpu.VMEM((own, K), f32),
+                pltpu.VMEM((own, K), link),
+                pltpu.VMEM((CHUNKS, GROUP, width, K), link),
                 pltpu.VMEM((CHUNKS, GROUP, width, K), f32),
-                pltpu.VMEM((CHUNKS, GROUP, width, K), f32),
-                pltpu.VMEM((CHUNKS, 2, width, K), f32),
-                pltpu.VMEM((CHUNKS, n_blocks, width, K), f32),
-                pltpu.VMEM((CHUNKS, GROUP, width, K), f32),
+                pltpu.VMEM((CHUNKS, 2, width, K), link),
+                pltpu.VMEM((CHUNKS, n_blocks, width, K), link),
+                pltpu.VMEM((CHUNKS, GROUP, width, K), link),
+                pltpu.VMEM((own, K), link),
                 dma((n_doc,)),
                 dma((n_doc,)),
                 dma((EITERS - 1, n_doc)),
@@ -429,7 +490,10 @@
                 collective_id=0, has_side_effects=True, vmem_limit_bytes=48 * 1024 * 1024
             ),
             name="topics",
-        )(local_beta, ids, cnt, block_slot, topic_prior[None], obs_precision, drift_var[None])
+        )(*[
+            pltpu.with_memory_space_constraint(a, pltpu.HBM)
+            for a in (local_beta, ids, cnt, block_slot, topic_prior[None], obs_precision, drift_var[None])
+        ])
         return (smoothed[None], doc_topics[None])
 
     in_specs = (P("tm", "doc", None), P("tm", "doc", None), P("tm", "doc", None), P(), P(), P(), P())

time: 79.8 us -> 62.7 us (0.79)
  Pallas kernels: 74.2 us -> 60.4 us
  local copies, waits for them, and re-layouts: 4.17 us -> 1.55 us
    pallas_call x1, Pallas kernels: 74.2 us -> 60.4 us  [body(): pl.pallas_call(functools.partial(kernel, n_tm, n_doc), out_shape=(jax.Sha...]
    unnamed x16 -> x2, local copies, waits for them, and re-layouts: 4.17 us -> 1.55 us
where the time goes in v4:
time: 62.7 us; the launch traced here: 62.6 us
  Pallas kernels  60.4 us (96%)
  local copies, waits for them, and re-layouts  1.55 us (2%)
  between operations  0.64 us (1%)
    pallas_call x1, Pallas kernels, body(): pl.pallas_call(functools.partial(kernel, n_tm, n_doc), out_shape=(jax.Sha...  60.4 us
    unnamed x2, local copies, waits for them, and re-layouts  1.55 us

profile of v4, /device:TPU:1, one launch (start us, length us, event | category | flops | bytes accessed | tf_op | source)
XLA Modules:
  0.0 62.6 jit_solution(6773317413766580425)
XLA Ops:
  0.6 60.4 %topics.1 = (f32[2048,128]{1,0:T(8,128)S(1)}, f32[4,128]{1,0:T(4,128)S(1)}) custom-call(f32[2048,128]{1,0:T(8,128)} %bitcast.9, s32[4,128]{1,0:T(4,128)} %bitcast.10, s32[4,128]{1,0:T(4,128)} %bitcast.11, s32[128]{0:T(128)} %slot_hbm.1, f32[1,128]{1,0:T(1,128)} %bitcast.12, f32[32,128]{1,0:T(8,128)} %prec_hbm.1, f32[1,128]{1,0:T(1,128)} %bitcast.13), custom_call_target="tpu_custom_call" | custom-call | tf_op jit(solution)/shard_map/topics/pallas_call | solution.py:440
  61.1 1.0 %copy.11 = f32[1,2048,128]{2,1,0:T(8,128)} copy(f32[1,2048,128]{2,1,0:T(8,128)S(1)} %bitcast.7) | data formatting | bytes 2097152
  62.1 0.6 copy.12

commit v5 on v4

--- a/solution.py
+++ b/solution.py
@@ -123,7 +123,7 @@
 
     peers = [(off, lax.rem(me + off, n_doc)) for off in far_first(n_doc)]
     mates = [(off, lax.rem(m + off, GROUP)) for off in range(1, GROUP)]
-    others = [(off, lax.rem(b + off, n_blocks)) for off in range(1, n_blocks)]
+    others = [(off, lax.rem(b + off, n_blocks)) for off in sorted(range(1, n_blocks), key=lambda off: abs(off - n_blocks // 2))]
 
     def mate_id(mate):
         return {"tm": b * GROUP + mate}
@@ -134,10 +134,10 @@
     barrier = pltpu.get_barrier_semaphore()
     for _, peer in peers:
         pl.semaphore_signal(barrier, inc=1, device_id={"doc": peer}, device_id_type=MESH)
+    for _, other in others:
+        pl.semaphore_signal(barrier, inc=1, device_id=other_id(other), device_id_type=MESH)
     for _, mate in mates:
         pl.semaphore_signal(barrier, inc=1, device_id=mate_id(mate), device_id_type=MESH)
-    for _, other in others:
-        pl.semaphore_signal(barrier, inc=1, device_id=other_id(other), device_id_type=MESH)
 
     loads = [
         pltpu.make_async_copy(source, held_here, load_sem.at[k])
@@ -217,7 +217,8 @@
 
     for s in range(n_doc):
         start = jnp.sum(land[s, 8 : 8 + dpd, :], axis=1, keepdims=True) / K
-        alpha[s * dpd : (s + 1) * dpd, :] = jnp.broadcast_to(start, (dpd, K))
+        row = (s % (n_doc // 2)) * dpd
+        alpha[s // (n_doc // 2), row : row + dpd, :] = jnp.broadcast_to(start, (dpd, K))
     alpha[...] = exp_digamma(prior + alpha[...])
 
     def look_up(s, _):
@@ -248,48 +249,50 @@
         expo[at, :] = jnp.exp(looked - jnp.max(looked, axis=1, keepdims=True))
         return 0
 
-    lax.fori_loop(0, n_doc, look_up, 0, unroll=2)
-
-    def sum_copy(sweep, off, peer, source):
-        return send(part.at[sweep], sums.at[sweep, source], sum_send.at[sweep, off], sum_recv.at[sweep, source], {"doc": peer})
+    lax.fori_loop(0, n_doc, look_up, 0, unroll=n_doc)
+
+    def sum_copy(sweep, half, off, peer, source):
+        turn = 2 * sweep + half
+        return send(
+            part.at[sweep, half], sums.at[sweep, source, half], sum_send.at[turn, off], sum_recv.at[turn, source], {"doc": peer}
+        )
 
     def end_copy(off, peer, source):
         return send(end_part.at[peer], end_sums.at[source], end_send.at[off], end_recv.at[source], {"doc": peer})
 
+    side = n_doc // 2
     for sweep in range(EITERS):
         last = sweep == EITERS - 1
-
-        def e_step(s, _, last=last, sweep=sweep):
-            for i in range(dpd):
-                row = s * dpd + i
-                at = pl.ds(pl.multiple_of(row * 128, 128), 128)
-                scaled = expo[at, :] * alpha[pl.ds(row, 1), :]
-                scaled = scaled * (scale[at, :] * (1.0 / jnp.sum(scaled, axis=1, keepdims=True)))
-                if last:
-                    end_part[s, i : i + 1, :] = jnp.sum(scaled, axis=0, keepdims=True)
-                    for f in range(FOLD):
-                        weighted[at, f * K : (f + 1) * K] = jnp.where(quarter[at, :] == float(f), scaled, 0.0).astype(
-                            jnp.bfloat16
-                        )
-                else:
-                    part[sweep, pl.ds(row, 1), :] = jnp.sum(scaled, axis=0, keepdims=True)
-            return 0
-
-        lax.fori_loop(0, n_doc, e_step, 0, unroll=2)
-        if not last:
-            for off, peer in peers:
-                sum_copy(sweep, off, peer, me).start()
-            sums[sweep, me] = part[sweep]
-            for off, peer in peers:
-                sum_copy(sweep, off, peer, peer).wait_recv()
-            whole = sums[sweep, 0]
-            for s in range(1, n_doc):
-                whole = whole + sums[sweep, s]
-            alpha[...] = exp_digamma(prior + whole)
-        else:
-            for off, peer in peers:
-                end_copy(off, peer, me).start()
-            end_sums[me] = end_part[me]
+        for half in range(2):
+            if sweep:
+                for off, peer in reversed(peers):
+                    sum_copy(sweep - 1, half, off, peer, peer).wait_recv()
+                whole = sums[sweep - 1, 0, half]
+                for s in range(1, n_doc):
+                    whole = whole + sums[sweep - 1, s, half]
+                alpha[half] = exp_digamma(prior + whole)
+
+            def e_step(s, _, last=last, sweep=sweep, half=half):
+                for i in range(dpd):
+                    row = s * dpd + i
+                    at = pl.ds(pl.multiple_of((half * side * dpd + row) * 128, 128), 128)
+                    scaled = expo[at, :] * alpha[half, pl.ds(row, 1), :]
+                    scaled = scaled * (scale[at, :] * (1.0 / jnp.sum(scaled, axis=1, keepdims=True)))
+                    if last:
+                        end_part[half * side + s, i : i + 1, :] = jnp.sum(scaled, axis=0, keepdims=True)
+                        for f in range(FOLD):
+                            weighted[at, f * K : (f + 1) * K] = jnp.where(quarter[at, :] == float(f), scaled, 0.0).astype(
+                                jnp.bfloat16
+                            )
+                    else:
+                        part[sweep, half, pl.ds(row, 1), :] = jnp.sum(scaled, axis=0, keepdims=True)
+                return 0
+
+            lax.fori_loop(0, side, e_step, 0, unroll=side)
+            if not last:
+                for off, peer in peers:
+                    sum_copy(sweep, half, off, peer, me).start()
+                sums[sweep, me, half] = part[sweep, half]
 
     def word_rows(mate, c):
         return pl.ds(pl.multiple_of(mate * span + c * width, width), width)
@@ -324,18 +327,15 @@
                 mate = f * spans + h
                 first = mate * span + c * width
                 whole = counts[h * width : (h + 1) * width, f * K : (f + 1) * K]
-                pseudo[first : first + width, :] = encode(beta_ref[first : first + width, :] + jnp.log1p(whole))
+                pseudo[first : first + width, :] = encode(beta_ref[first : first + width, :] + jnp.log(1.0 + whole))
 
                 @pl.when(mate != m)
                 def _(mate=mate, c=c):
                     in_copy(c, mate, m).start()
 
     for off, peer in peers:
-        end_copy(off, peer, peer).wait_recv()
-    whole = end_sums[0]
-    for s in range(1, n_doc):
-        whole = whole + end_sums[s]
-    topics_ref[...] = prior + whole
+        end_copy(off, peer, me).start()
+    end_sums[me] = end_part[me]
 
     first_year = b * GROUP
     g = [gain[pl.ds(first_year + i, 1), :] for i in range(GROUP)]
@@ -366,6 +366,12 @@
         which = jnp.where(other > b, 0, 1)
         return send(mid_out.at[c, which], mid_in.at[c, source], mid_send.at[c, off], mid_recv.at[c, source], other_id(other))
 
+    for off, peer in peers:
+        msg_copy(off, peer, me).wait_send()
+        for sweep in range(EITERS - 1):
+            for half in range(2):
+                sum_copy(sweep, half, off, peer, me).wait_send()
+
     for c in range(CHUNKS):
         years_in[c, m] = pseudo[word_rows(m, c), :]
         mid_in[c, b] = jnp.zeros((width, K), jnp.int16)
@@ -386,6 +392,19 @@
         for off, other in others:
             mid_copy(c, off, other, b).start()
 
+    for off, peer in peers:
+        end_copy(off, peer, peer).wait_recv()
+    whole = end_sums[0]
+    for s in range(1, n_doc):
+        whole = whole + end_sums[s]
+    topics_ref[...] = prior + whole
+
+    for off, peer in peers:
+        end_copy(off, peer, me).wait_send()
+    for c in range(CHUNKS):
+        for off, mate in mates:
+            in_copy(c, mate, m).wait_send()
+
     def out_copy(c, mate, source):
         return send(
             years_out.at[c, mate], coded.at[word_rows(source, c), :], out_send.at[c, mate], out_recv.at[c, source], mate_id(mate)
@@ -406,20 +425,15 @@
         out_ref[word_rows(m, c), :] = decode(years_out[c, m])
 
     for c in range(CHUNKS):
+        for off, other in others:
+            mid_copy(c, off, other, b).wait_send()
+    for c in range(CHUNKS):
         for off, mate in mates:
             out_copy(c, mate, mate).wait_recv()
             out_ref[word_rows(mate, c), :] = decode(coded[word_rows(mate, c), :])
-    for off, peer in peers:
-        msg_copy(off, peer, me).wait_send()
-        for sweep in range(EITERS - 1):
-            sum_copy(sweep, off, peer, me).wait_send()
-        end_copy(off, peer, me).wait_send()
     for c in range(CHUNKS):
         for off, mate in mates:
-            in_copy(c, mate, m).wait_send()
             out_copy(c, mate, m).wait_send()
-        for off, other in others:
-            mid_copy(c, off, other, b).wait_send()
 
 
 def vmem():
@@ -458,9 +472,9 @@
                 pltpu.VMEM((n_doc * held, K), f32),
                 pltpu.VMEM((n_doc * held, K), f32),
                 pltpu.VMEM((n_doc * held, FOLD * K), bf16),
-                pltpu.VMEM((n_doc * dpd, K), f32),
-                pltpu.VMEM((EITERS - 1, n_doc * dpd, K), f32),
-                pltpu.VMEM((EITERS - 1, n_doc, n_doc * dpd, K), f32),
+                pltpu.VMEM((2, n_doc // 2 * dpd, K), f32),
+                pltpu.VMEM((EITERS - 1, 2, n_doc // 2 * dpd, K), f32),
+                pltpu.VMEM((EITERS - 1, n_doc, 2, n_doc // 2 * dpd, K), f32),
                 pltpu.VMEM((n_doc, dpd, K), f32),
                 pltpu.VMEM((n_doc, dpd, K), f32),
                 pltpu.VMEM((n_tm, K), f32),
@@ -475,8 +489,8 @@
                 pltpu.VMEM((own, K), link),
                 dma((n_doc,)),
                 dma((n_doc,)),
-                dma((EITERS - 1, n_doc)),
-                dma((EITERS - 1, n_doc)),
+                dma((2 * EITERS - 2, n_doc)),
+                dma((2 * EITERS - 2, n_doc)),
                 dma((n_doc,)),
                 dma((n_doc,)),
                 dma((CHUNKS, GROUP)),

time: 62.7 us -> 58.3 us (0.930)
  Pallas kernels: 60.4 us -> 56 us
    pallas_call x1, Pallas kernels: 60.4 us -> 56 us  [body(): pl.pallas_call(functools.partial(kernel, n_tm, n_doc), out_shape=(jax.Sha...]
where the time goes in v5:
time: 58.3 us; the launch traced here: 58.2 us
  Pallas kernels  56 us (96%)
  local copies, waits for them, and re-layouts  1.55 us (3%)
  between operations  0.64 us (1%)
    pallas_call x1, Pallas kernels, body(): pl.pallas_call(functools.partial(kernel, n_tm, n_doc), out_shape=(jax.Sha...  56 us
    unnamed x2, local copies, waits for them, and re-layouts  1.55 us

profile of v5, /device:TPU:1, one launch (start us, length us, event | category | flops | bytes accessed | tf_op | source)
XLA Modules:
  0.0 58.2 jit_solution(7442938022560659141)
XLA Ops:
  0.6 56.0 %topics.1 = (f32[2048,128]{1,0:T(8,128)S(1)}, f32[4,128]{1,0:T(4,128)S(1)}) custom-call(f32[2048,128]{1,0:T(8,128)} %bitcast.9, s32[4,128]{1,0:T(4,128)} %bitcast.10, s32[4,128]{1,0:T(4,128)} %bitcast.11, s32[128]{0:T(128)} %slot_hbm.1, f32[1,128]{1,0:T(1,128)} %bitcast.12, f32[32,128]{1,0:T(8,128)} %prec_hbm.1, f32[1,128]{1,0:T(1,128)} %bitcast.13), custom_call_target="tpu_custom_call" | custom-call | tf_op jit(solution)/shard_map/topics/pallas_call | solution.py:454
  56.6 1.0 %copy.11 = f32[1,2048,128]{2,1,0:T(8,128)} copy(f32[1,2048,128]{2,1,0:T(8,128)S(1)} %bitcast.7) | data formatting | bytes 2097152
  57.6 0.6 copy.12

commit v6 on v5

--- a/solution.py
+++ b/solution.py
@@ -51,8 +51,13 @@
     )
 
 
-def far_first(count):
-    return sorted(range(1, count), key=lambda off: abs(off - count // 2) + 2 * (1 - off % 2))
+def flipped(index, mask):
+    bit = 1
+    while bit <= mask:
+        if mask & bit:
+            index = index + bit - 2 * bit * lax.rem(index // bit, 2)
+        bit *= 2
+    return index
 
 
 def kernel(
@@ -65,7 +70,7 @@
     prior_hbm,
     prec_hbm,
     drift_hbm,
-    out_ref,
+    coded,
     topics_ref,
     beta_ref,
     ids_ref,
@@ -82,6 +87,7 @@
     scale,
     quarter,
     weighted,
+    counts,
     alpha,
     part,
     sums,
@@ -96,7 +102,6 @@
     mid_out,
     mid_in,
     years_out,
-    coded,
     msg_send,
     msg_recv,
     sum_send,
@@ -121,9 +126,12 @@
     span = own // GROUP
     width = span // CHUNKS
 
-    peers = [(off, lax.rem(me + off, n_doc)) for off in far_first(n_doc)]
-    mates = [(off, lax.rem(m + off, GROUP)) for off in range(1, GROUP)]
-    others = [(off, lax.rem(b + off, n_blocks)) for off in sorted(range(1, n_blocks), key=lambda off: abs(off - n_blocks // 2))]
+    def partners(index, count, order):
+        return [(mask, flipped(index, mask)) for mask in order if mask < count]
+
+    peers = partners(me, n_doc, (5, 3, 7, 4, 1, 2, 6))
+    mates = partners(m, GROUP, (7, 6, 5, 4, 3, 2, 1))
+    others = partners(b, n_blocks, (2, 1, 3))
 
     def mate_id(mate):
         return {"tm": b * GROUP + mate}
@@ -249,8 +257,6 @@
         expo[at, :] = jnp.exp(looked - jnp.max(looked, axis=1, keepdims=True))
         return 0
 
-    lax.fori_loop(0, n_doc, look_up, 0, unroll=n_doc)
-
     def sum_copy(sweep, half, off, peer, source):
         turn = 2 * sweep + half
         return send(
@@ -260,11 +266,54 @@
     def end_copy(off, peer, source):
         return send(end_part.at[peer], end_sums.at[source], end_send.at[off], end_recv.at[source], {"doc": peer})
 
+    def word_rows(mate, c):
+        return pl.ds(pl.multiple_of(mate * span + c * width, width), width)
+
+    def in_copy(c, mate, source):
+        return send(
+            pseudo.at[word_rows(mate, c), :], years_in.at[c, source], in_send.at[c, mate], in_recv.at[c, source], mate_id(mate)
+        )
+
     side = n_doc // 2
+    spans = fold // span
+    words = lax.broadcasted_iota(jnp.int32, (width, 128), 0).astype(jnp.float32)
+
+    def tally(half, c):
+        marks = []
+        for s in range(half * side, (half + 1) * side):
+            rest = land[s, 0:dpd, :] - base
+            rest = rest - float(fold) * jnp.floor(rest * (1.0 / fold))
+            for i in range(dpd):
+                marks.append(
+                    jnp.concatenate(
+                        [
+                            (words + float(h * span + c * width) == rest[i : i + 1, :]).astype(jnp.bfloat16)
+                            for h in range(spans)
+                        ],
+                        axis=0,
+                    )
+                )
+        docs = slice(half * side * held, (half + 1) * side * held)
+        found = jnp.dot(jnp.concatenate(marks, axis=1), weighted[docs, :], preferred_element_type=jnp.float32)
+        if half == 0:
+            counts[c] = found
+            return
+        for h in range(spans):
+            for f in range(FOLD):
+                mate = f * spans + h
+                first = mate * span + c * width
+                rows, columns = slice(h * width, (h + 1) * width), slice(f * K, (f + 1) * K)
+                whole = counts[c, rows, columns] + found[rows, columns]
+                pseudo[first : first + width, :] = encode(beta_ref[first : first + width, :] + jnp.log(1.0 + whole))
+        for _, mate in mates:
+            in_copy(c, mate, m).start()
+
     for sweep in range(EITERS):
         last = sweep == EITERS - 1
         for half in range(2):
-            if sweep:
+            if sweep == 0:
+                lax.fori_loop(half * side, (half + 1) * side, look_up, 0, unroll=side)
+            else:
                 for off, peer in reversed(peers):
                     sum_copy(sweep - 1, half, off, peer, peer).wait_recv()
                 whole = sums[sweep - 1, 0, half]
@@ -293,45 +342,9 @@
                 for off, peer in peers:
                     sum_copy(sweep, half, off, peer, me).start()
                 sums[sweep, me, half] = part[sweep, half]
-
-    def word_rows(mate, c):
-        return pl.ds(pl.multiple_of(mate * span + c * width, width), width)
-
-    def in_copy(c, mate, source):
-        return send(
-            pseudo.at[word_rows(mate, c), :], years_in.at[c, source], in_send.at[c, mate], in_recv.at[c, source], mate_id(mate)
-        )
-
-    spans = fold // span
-    rests = []
-    for s in range(n_doc):
-        col = land[s, 0:dpd, :] - base
-        rests.append(col - float(fold) * jnp.floor(col * (1.0 / fold)))
-    words = lax.broadcasted_iota(jnp.int32, (width, 128), 0).astype(jnp.float32)
-    for c in range(CHUNKS):
-        marks = []
-        for s in range(n_doc):
-            for i in range(dpd):
-                marks.append(
-                    jnp.concatenate(
-                        [
-                            (words + float(h * span + c * width) == rests[s][i : i + 1, :]).astype(jnp.bfloat16)
-                            for h in range(spans)
-                        ],
-                        axis=0,
-                    )
-                )
-        counts = jnp.dot(jnp.concatenate(marks, axis=1), weighted[...], preferred_element_type=jnp.float32)
-        for h in range(spans):
-            for f in range(FOLD):
-                mate = f * spans + h
-                first = mate * span + c * width
-                whole = counts[h * width : (h + 1) * width, f * K : (f + 1) * K]
-                pseudo[first : first + width, :] = encode(beta_ref[first : first + width, :] + jnp.log(1.0 + whole))
-
-                @pl.when(mate != m)
-                def _(mate=mate, c=c):
-                    in_copy(c, mate, m).start()
+            else:
+                for c in range(CHUNKS):
+                    tally(half, c)
 
     for off, peer in peers:
         end_copy(off, peer, me).start()
@@ -422,7 +435,7 @@
             years_out[c, i] = encode(local[c, i] + (w[i] * keep[i]) * ahead + ((1.0 - w[i]) * hold[i + 1]) * behind)
         for off, mate in mates:
             out_copy(c, mate, m).start()
-        out_ref[word_rows(m, c), :] = decode(years_out[c, m])
+        coded[word_rows(m, c), :] = years_out[c, m]
 
     for c in range(CHUNKS):
         for off, other in others:
@@ -430,7 +443,6 @@
     for c in range(CHUNKS):
         for off, mate in mates:
             out_copy(c, mate, mate).wait_recv()
-            out_ref[word_rows(mate, c), :] = decode(coded[word_rows(mate, c), :])
     for c in range(CHUNKS):
         for off, mate in mates:
             out_copy(c, mate, m).wait_send()
@@ -453,7 +465,7 @@
         dma = pltpu.SemaphoreType.DMA
         smoothed, doc_topics = pl.pallas_call(
             functools.partial(kernel, n_tm, n_doc),
-            out_shape=(jax.ShapeDtypeStruct((own, K), f32), jax.ShapeDtypeStruct((dpd, K), f32)),
+            out_shape=(jax.ShapeDtypeStruct((own, K), link), jax.ShapeDtypeStruct((dpd, K), f32)),
             in_specs=[pl.BlockSpec(memory_space=pltpu.HBM)] * 7,
             out_specs=(vmem(), vmem()),
             scratch_shapes=[
@@ -472,6 +484,7 @@
                 pltpu.VMEM((n_doc * held, K), f32),
                 pltpu.VMEM((n_doc * held, K), f32),
                 pltpu.VMEM((n_doc * held, FOLD * K), bf16),
+                pltpu.VMEM((CHUNKS, own // FOLD // CHUNKS, FOLD * K), f32),
                 pltpu.VMEM((2, n_doc // 2 * dpd, K), f32),
                 pltpu.VMEM((EITERS - 1, 2, n_doc // 2 * dpd, K), f32),
                 pltpu.VMEM((EITERS - 1, n_doc, 2, n_doc // 2 * dpd, K), f32),
@@ -486,7 +499,6 @@
                 pltpu.VMEM((CHUNKS, 2, width, K), link),
                 pltpu.VMEM((CHUNKS, n_blocks, width, K), link),
                 pltpu.VMEM((CHUNKS, GROUP, width, K), link),
-                pltpu.VMEM((own, K), link),
                 dma((n_doc,)),
                 dma((n_doc,)),
                 dma((2 * EITERS - 2, n_doc)),
@@ -508,7 +520,7 @@
             pltpu.with_memory_space_constraint(a, pltpu.HBM)
             for a in (local_beta, ids, cnt, block_slot, topic_prior[None], obs_precision, drift_var[None])
         ])
-        return (smoothed[None], doc_topics[None])
+        return (decode(smoothed)[None], doc_topics[None])
 
     in_specs = (P("tm", "doc", None), P("tm", "doc", None), P("tm", "doc", None), P(), P(), P(), P())
     out_specs = (P("tm", "doc", None), P("tm", "doc", None))

time: 58.3 us -> 57.7 us (0.990)
  other arithmetic: 0 us -> 1.42 us
  Pallas kernels: 56 us -> 55 us
  local copies, waits for them, and re-layouts: 1.55 us -> 0.58 us
    broadcast_in_dim x0 -> x1, other arithmetic: none -> 1.42 us  [body(): return (decode(smoothed)[None], doc_topics[None])]
    pallas_call x1, Pallas kernels: 56 us -> 55 us  [body(): pl.pallas_call(functools.partial(kernel, n_tm, n_doc), out_shape=(jax.Sha...]
    unnamed x2 -> x1, local copies, waits for them, and re-layouts: 1.55 us -> 0.58 us
where the time goes in v6:
time: 57.7 us; the launch traced here: 57.6 us
  Pallas kernels  55 us (95%)
  other arithmetic  1.42 us (2%)
  between operations  0.64 us (1%)
  local copies, waits for them, and re-layouts  0.58 us (1%)
    pallas_call x1, Pallas kernels, body(): pl.pallas_call(functools.partial(kernel, n_tm, n_doc), out_shape=(jax.Sha...  55 us
    broadcast_in_dim x1, other arithmetic, body(): return (decode(smoothed)[None], doc_topics[None])  1.42 us

profile of v6, /device:TPU:1, one launch (start us, length us, event | category | flops | bytes accessed | tf_op | source)
XLA Modules:
  0.0 57.6 jit_solution(6748112697135606943)
XLA Ops:
  0.6 55.0 %topics.1 = (s16[2048,128]{1,0:T(8,128)(2,1)S(1)}, f32[4,128]{1,0:T(4,128)S(1)}) custom-call(f32[2048,128]{1,0:T(8,128)} %bitcast.9, s32[4,128]{1,0:T(4,128)} %bitcast.10, s32[4,128]{1,0:T(4,128)} %bitcast.11, s32[128]{0:T(128)} %slot_hbm.1, f32[1,128]{1,0:T(1,128)} %bitcast.12, f32[32,128]{1,0:T(8,128)} %prec_hbm.1, f32[1,128]{1,0:T(1,128)} %bitcast.13), custom_call_target="tpu_custom_call" | custom-call | tf_op jit(solution)/shard_map/topics/pallas_call | solution.py:466
  55.6 1.4 %fusion.4 = f32[1,2048,128]{2,1,0:T(8,128)} fusion(s16[2048,128]{1,0:T(8,128)(2,1)S(1)} %get-tuple-element.4), kind=kLoop, calls=%fused_computation.7 | loop fusion | flops 2097152 | bytes 1572864 | tf_op jit(solution)/shard_map/broadcast_in_dim | solution.py:523
  57.0 0.6 %copy.10 = f32[1,4,128]{2,1,0:T(4,128)} copy(f32[1,4,128]{2,1,0:T(4,128)S(1)} %bitcast.8) | data formatting | bytes 4096

commit v7 on v6

--- a/solution.py
+++ b/solution.py
@@ -13,7 +13,8 @@
 EITERS = 4
 GROUP = 8
 FOLD = 4
-CHUNKS = 2
+PARTS = 2
+CHUNKS = 4
 INIT_VAR = 4.0
 MESH = pl.DeviceIdType.MESH
 
@@ -70,7 +71,7 @@
     prior_hbm,
     prec_hbm,
     drift_hbm,
-    coded,
+    out_ref,
     topics_ref,
     beta_ref,
     ids_ref,
@@ -102,6 +103,7 @@
     mid_out,
     mid_in,
     years_out,
+    coded,
     msg_send,
     msg_recv,
     sum_send,
@@ -117,6 +119,8 @@
 ):
     me = lax.axis_index("doc")
     t = lax.axis_index("tm")
+    parts = min(PARTS, n_doc)
+    side = n_doc // parts
     n_blocks = n_tm // GROUP
     b = t // GROUP
     m = lax.rem(t, GROUP)
@@ -136,14 +140,19 @@
     def mate_id(mate):
         return {"tm": b * GROUP + mate}
 
-    def other_id(other):
-        return {"tm": other * GROUP + m}
+    far_bit = GROUP // 2
+
+    def span_of(member):
+        return member + (b // 2) * (far_bit - 2 * far_bit * (member // far_bit))
+
+    def other_id(mask, other):
+        return {"tm": other * GROUP + (flipped(m, far_bit) if mask & 2 else m)}
 
     barrier = pltpu.get_barrier_semaphore()
     for _, peer in peers:
         pl.semaphore_signal(barrier, inc=1, device_id={"doc": peer}, device_id_type=MESH)
-    for _, other in others:
-        pl.semaphore_signal(barrier, inc=1, device_id=other_id(other), device_id_type=MESH)
+    for mask, other in others:
+        pl.semaphore_signal(barrier, inc=1, device_id=other_id(mask, other), device_id_type=MESH)
     for _, mate in mates:
         pl.semaphore_signal(barrier, inc=1, device_id=mate_id(mate), device_id_type=MESH)
 
@@ -225,8 +234,8 @@
 
     for s in range(n_doc):
         start = jnp.sum(land[s, 8 : 8 + dpd, :], axis=1, keepdims=True) / K
-        row = (s % (n_doc // 2)) * dpd
-        alpha[s // (n_doc // 2), row : row + dpd, :] = jnp.broadcast_to(start, (dpd, K))
+        row = (s % side) * dpd
+        alpha[s // side, row : row + dpd, :] = jnp.broadcast_to(start, (dpd, K))
     alpha[...] = exp_digamma(prior + alpha[...])
 
     def look_up(s, _):
@@ -257,30 +266,29 @@
         expo[at, :] = jnp.exp(looked - jnp.max(looked, axis=1, keepdims=True))
         return 0
 
-    def sum_copy(sweep, half, off, peer, source):
-        turn = 2 * sweep + half
+    def sum_copy(sweep, part_no, off, peer, source):
+        turn = parts * sweep + part_no
         return send(
-            part.at[sweep, half], sums.at[sweep, source, half], sum_send.at[turn, off], sum_recv.at[turn, source], {"doc": peer}
+            part.at[sweep, part_no], sums.at[sweep, source, part_no], sum_send.at[turn, off], sum_recv.at[turn, source], {"doc": peer}
         )
 
     def end_copy(off, peer, source):
         return send(end_part.at[peer], end_sums.at[source], end_send.at[off], end_recv.at[source], {"doc": peer})
 
     def word_rows(mate, c):
-        return pl.ds(pl.multiple_of(mate * span + c * width, width), width)
+        return pl.ds(pl.multiple_of(span_of(mate) * span + c * width, width), width)
 
     def in_copy(c, mate, source):
         return send(
             pseudo.at[word_rows(mate, c), :], years_in.at[c, source], in_send.at[c, mate], in_recv.at[c, source], mate_id(mate)
         )
 
-    side = n_doc // 2
     spans = fold // span
     words = lax.broadcasted_iota(jnp.int32, (width, 128), 0).astype(jnp.float32)
 
-    def tally(half, c):
+    def tally(part_no, c):
         marks = []
-        for s in range(half * side, (half + 1) * side):
+        for s in range(part_no * side, (part_no + 1) * side):
             rest = land[s, 0:dpd, :] - base
             rest = rest - float(fold) * jnp.floor(rest * (1.0 / fold))
             for i in range(dpd):
@@ -293,10 +301,13 @@
                         axis=0,
                     )
                 )
-        docs = slice(half * side * held, (half + 1) * side * held)
+        docs = slice(part_no * side * held, (part_no + 1) * side * held)
         found = jnp.dot(jnp.concatenate(marks, axis=1), weighted[docs, :], preferred_element_type=jnp.float32)
-        if half == 0:
+        if part_no == 0:
             counts[c] = found
+        elif part_no < parts - 1:
+            counts[c] += found
+        if part_no < parts - 1:
             return
         for h in range(spans):
             for f in range(FOLD):
@@ -310,41 +321,41 @@
 
     for sweep in range(EITERS):
         last = sweep == EITERS - 1
-        for half in range(2):
+        for part_no in range(parts):
             if sweep == 0:
-                lax.fori_loop(half * side, (half + 1) * side, look_up, 0, unroll=side)
+                lax.fori_loop(part_no * side, (part_no + 1) * side, look_up, 0, unroll=side)
             else:
                 for off, peer in reversed(peers):
-                    sum_copy(sweep - 1, half, off, peer, peer).wait_recv()
-                whole = sums[sweep - 1, 0, half]
+                    sum_copy(sweep - 1, part_no, off, peer, peer).wait_recv()
+                whole = sums[sweep - 1, 0, part_no]
                 for s in range(1, n_doc):
-                    whole = whole + sums[sweep - 1, s, half]
-                alpha[half] = exp_digamma(prior + whole)
-
-            def e_step(s, _, last=last, sweep=sweep, half=half):
+                    whole = whole + sums[sweep - 1, s, part_no]
+                alpha[part_no] = exp_digamma(prior + whole)
+
+            def e_step(s, _, last=last, sweep=sweep, part_no=part_no):
                 for i in range(dpd):
                     row = s * dpd + i
-                    at = pl.ds(pl.multiple_of((half * side * dpd + row) * 128, 128), 128)
-                    scaled = expo[at, :] * alpha[half, pl.ds(row, 1), :]
+                    at = pl.ds(pl.multiple_of((part_no * side * dpd + row) * 128, 128), 128)
+                    scaled = expo[at, :] * alpha[part_no, pl.ds(row, 1), :]
                     scaled = scaled * (scale[at, :] * (1.0 / jnp.sum(scaled, axis=1, keepdims=True)))
                     if last:
-                        end_part[half * side + s, i : i + 1, :] = jnp.sum(scaled, axis=0, keepdims=True)
+                        end_part[part_no * side + s, i : i + 1, :] = jnp.sum(scaled, axis=0, keepdims=True)
                         for f in range(FOLD):
                             weighted[at, f * K : (f + 1) * K] = jnp.where(quarter[at, :] == float(f), scaled, 0.0).astype(
                                 jnp.bfloat16
                             )
                     else:
-                        part[sweep, half, pl.ds(row, 1), :] = jnp.sum(scaled, axis=0, keepdims=True)
+                        part[sweep, part_no, pl.ds(row, 1), :] = jnp.sum(scaled, axis=0, keepdims=True)
                 return 0
 
             lax.fori_loop(0, side, e_step, 0, unroll=side)
             if not last:
                 for off, peer in peers:
-                    sum_copy(sweep, half, off, peer, me).start()
-                sums[sweep, me, half] = part[sweep, half]
+                    sum_copy(sweep, part_no, off, peer, me).start()
+                sums[sweep, me, part_no] = part[sweep, part_no]
             else:
                 for c in range(CHUNKS):
-                    tally(half, c)
+                    tally(part_no, c)
 
     for off, peer in peers:
         end_copy(off, peer, me).start()
@@ -377,13 +388,13 @@
 
     def mid_copy(c, off, other, source):
         which = jnp.where(other > b, 0, 1)
-        return send(mid_out.at[c, which], mid_in.at[c, source], mid_send.at[c, off], mid_recv.at[c, source], other_id(other))
+        return send(mid_out.at[c, which], mid_in.at[c, source], mid_send.at[c, off], mid_recv.at[c, source], other_id(off, other))
 
     for off, peer in peers:
         msg_copy(off, peer, me).wait_send()
         for sweep in range(EITERS - 1):
-            for half in range(2):
-                sum_copy(sweep, half, off, peer, me).wait_send()
+            for part_no in range(parts):
+                sum_copy(sweep, part_no, off, peer, me).wait_send()
 
     for c in range(CHUNKS):
         years_in[c, m] = pseudo[word_rows(m, c), :]
@@ -435,7 +446,7 @@
             years_out[c, i] = encode(local[c, i] + (w[i] * keep[i]) * ahead + ((1.0 - w[i]) * hold[i + 1]) * behind)
         for off, mate in mates:
             out_copy(c, mate, m).start()
-        coded[word_rows(m, c), :] = years_out[c, m]
+        out_ref[word_rows(m, c), :] = decode(years_out[c, m])
 
     for c in range(CHUNKS):
         for off, other in others:
@@ -443,6 +454,7 @@
     for c in range(CHUNKS):
         for off, mate in mates:
             out_copy(c, mate, mate).wait_recv()
+            out_ref[word_rows(mate, c), :] = decode(coded[word_rows(mate, c), :])
     for c in range(CHUNKS):
         for off, mate in mates:
             out_copy(c, mate, m).wait_send()
@@ -461,11 +473,13 @@
         held = dpd * 128
         width = own // GROUP // CHUNKS
         n_blocks = n_tm // GROUP
+        parts = min(PARTS, n_doc)
+        lot = n_doc // parts * dpd
         f32, bf16, link = jnp.float32, jnp.bfloat16, jnp.int16
         dma = pltpu.SemaphoreType.DMA
         smoothed, doc_topics = pl.pallas_call(
             functools.partial(kernel, n_tm, n_doc),
-            out_shape=(jax.ShapeDtypeStruct((own, K), link), jax.ShapeDtypeStruct((dpd, K), f32)),
+            out_shape=(jax.ShapeDtypeStruct((own, K), f32), jax.ShapeDtypeStruct((dpd, K), f32)),
             in_specs=[pl.BlockSpec(memory_space=pltpu.HBM)] * 7,
             out_specs=(vmem(), vmem()),
             scratch_shapes=[
@@ -485,9 +499,9 @@
                 pltpu.VMEM((n_doc * held, K), f32),
                 pltpu.VMEM((n_doc * held, FOLD * K), bf16),
                 pltpu.VMEM((CHUNKS, own // FOLD // CHUNKS, FOLD * K), f32),
-                pltpu.VMEM((2, n_doc // 2 * dpd, K), f32),
-                pltpu.VMEM((EITERS - 1, 2, n_doc // 2 * dpd, K), f32),
-                pltpu.VMEM((EITERS - 1, n_doc, 2, n_doc // 2 * dpd, K), f32),
+                pltpu.VMEM((parts, lot, K), f32),
+                pltpu.VMEM((EITERS - 1, parts, lot, K), f32),
+                pltpu.VMEM((EITERS - 1, n_doc, parts, lot, K), f32),
                 pltpu.VMEM((n_doc, dpd, K), f32),
                 pltpu.VMEM((n_doc, dpd, K), f32),
                 pltpu.VMEM((n_tm, K), f32),
@@ -499,10 +513,11 @@
                 pltpu.VMEM((CHUNKS, 2, width, K), link),
                 pltpu.VMEM((CHUNKS, n_blocks, width, K), link),
                 pltpu.VMEM((CHUNKS, GROUP, width, K), link),
+                pltpu.VMEM((own, K), link),
                 dma((n_doc,)),
                 dma((n_doc,)),
-                dma((2 * EITERS - 2, n_doc)),
-                dma((2 * EITERS - 2, n_doc)),
+                dma((parts * (EITERS - 1), n_doc)),
+                dma((parts * (EITERS - 1), n_doc)),
                 dma((n_doc,)),
                 dma((n_doc,)),
                 dma((CHUNKS, GROUP)),
@@ -520,7 +535,7 @@
             pltpu.with_memory_space_constraint(a, pltpu.HBM)
             for a in (local_beta, ids, cnt, block_slot, topic_prior[None], obs_precision, drift_var[None])
         ])
-        return (decode(smoothed)[None], doc_topics[None])
+        return (smoothed[None], doc_topics[None])
 
     in_specs = (P("tm", "doc", None), P("tm", "doc", None), P("tm", "doc", None), P(), P(), P(), P())
     out_specs = (P("tm", "doc", None), P("tm", "doc", None))

time: 57.7 us -> 56.5 us (0.979)
  other arithmetic: 1.42 us -> 0 us
  local copies, waits for them, and re-layouts: 0.58 us -> 1.55 us
  Pallas kernels: 55 us -> 54.2 us
    broadcast_in_dim x1 -> x0, other arithmetic: 1.42 us -> none  [body(): return (decode(smoothed)[None], doc_topics[None])]
    unnamed x1 -> x2, local copies, waits for them, and re-layouts: 0.58 us -> 1.55 us
    pallas_call x1, Pallas kernels: 55 us -> 54.2 us  [body(): pl.pallas_call(functools.partial(kernel, n_tm, n_doc), out_shape=(jax.Sha...]
where the time goes in v7:
time: 56.5 us; the launch traced here: 56.4 us
  Pallas kernels  54.2 us (96%)
  local copies, waits for them, and re-layouts  1.55 us (3%)
  between operations  0.64 us (1%)
    pallas_call x1, Pallas kernels, body(): pl.pallas_call(functools.partial(kernel, n_tm, n_doc), out_shape=(jax.Sha...  54.2 us
    unnamed x2, local copies, waits for them, and re-layouts  1.55 us

profile of v7, /device:TPU:1, one launch (start us, length us, event | category | flops | bytes accessed | tf_op | source)
XLA Modules:
  0.0 56.4 jit_solution(16119756415705376897)
XLA Ops:
  0.6 54.2 %topics.1 = (f32[2048,128]{1,0:T(8,128)S(1)}, f32[4,128]{1,0:T(4,128)S(1)}) custom-call(f32[2048,128]{1,0:T(8,128)} %bitcast.9, s32[4,128]{1,0:T(4,128)} %bitcast.10, s32[4,128]{1,0:T(4,128)} %bitcast.11, s32[128]{0:T(128)} %slot_hbm.1, f32[1,128]{1,0:T(1,128)} %bitcast.12, f32[32,128]{1,0:T(8,128)} %prec_hbm.1, f32[1,128]{1,0:T(1,128)} %bitcast.13), custom_call_target="tpu_custom_call" | custom-call | tf_op jit(solution)/shard_map/topics/pallas_call | solution.py:480
  54.8 1.0 %copy.11 = f32[1,2048,128]{2,1,0:T(8,128)} copy(f32[1,2048,128]{2,1,0:T(8,128)S(1)} %bitcast.7) | data formatting | bytes 2097152
  55.8 0.6 %copy.12 = f32[1,4,128]{2,1,0:T(4,128)} copy(f32[1,4,128]{2,1,0:T(4,128)S(1)} %bitcast.8) | data formatting | bytes 4096

commit v8 on v7

--- a/solution.py
+++ b/solution.py
@@ -416,19 +416,6 @@
         for off, other in others:
             mid_copy(c, off, other, b).start()
 
-    for off, peer in peers:
-        end_copy(off, peer, peer).wait_recv()
-    whole = end_sums[0]
-    for s in range(1, n_doc):
-        whole = whole + end_sums[s]
-    topics_ref[...] = prior + whole
-
-    for off, peer in peers:
-        end_copy(off, peer, me).wait_send()
-    for c in range(CHUNKS):
-        for off, mate in mates:
-            in_copy(c, mate, m).wait_send()
-
     def out_copy(c, mate, source):
         return send(
             years_out.at[c, mate], coded.at[word_rows(source, c), :], out_send.at[c, mate], out_recv.at[c, source], mate_id(mate)
@@ -448,6 +435,18 @@
             out_copy(c, mate, m).start()
         out_ref[word_rows(m, c), :] = decode(years_out[c, m])
 
+    for off, peer in peers:
+        end_copy(off, peer, peer).wait_recv()
+    whole = end_sums[0]
+    for s in range(1, n_doc):
+        whole = whole + end_sums[s]
+    topics_ref[...] = prior + whole
+
+    for off, peer in peers:
+        end_copy(off, peer, me).wait_send()
+    for c in range(CHUNKS):
+        for off, mate in mates:
+            in_copy(c, mate, m).wait_send()
     for c in range(CHUNKS):
         for off, other in others:
             mid_copy(c, off, other, b).wait_send()

time: 56.5 us -> 56.5 us (level)
  no operation moved by 1% of the time
where the time goes in v8:
time: 56.5 us; the launch traced here: 56.4 us
  Pallas kernels  54.2 us (96%)
  local copies, waits for them, and re-layouts  1.55 us (3%)
  between operations  0.64 us (1%)
    pallas_call x1, Pallas kernels, body(): pl.pallas_call(functools.partial(kernel, n_tm, n_doc), out_shape=(jax.Sha...  54.2 us
    unnamed x2, local copies, waits for them, and re-layouts  1.55 us

profile of v8, /device:TPU:1, one launch (start us, length us, event | category | flops | bytes accessed | tf_op | source)
XLA Modules:
  0.0 56.4 jit_solution(9476257077273353845)
XLA Ops:
  0.6 54.2 %topics.1 = (f32[2048,128]{1,0:T(8,128)S(1)}, f32[4,128]{1,0:T(4,128)S(1)}) custom-call(f32[2048,128]{1,0:T(8,128)} %bitcast.9, s32[4,128]{1,0:T(4,128)} %bitcast.10, s32[4,128]{1,0:T(4,128)} %bitcast.11, s32[128]{0:T(128)} %slot_hbm.1, f32[1,128]{1,0:T(1,128)} %bitcast.12, f32[32,128]{1,0:T(8,128)} %prec_hbm.1, f32[1,128]{1,0:T(1,128)} %bitcast.13), custom_call_target="tpu_custom_call" | custom-call | tf_op jit(solution)/shard_map/topics/pallas_call | solution.py:479
  54.8 1.0 %copy.11 = f32[1,2048,128]{2,1,0:T(8,128)} copy(f32[1,2048,128]{2,1,0:T(8,128)S(1)} %bitcast.7) | data formatting | bytes 2097152
  55.8 0.6 %copy.12 = f32[1,4,128]{2,1,0:T(4,128)} copy(f32[1,4,128]{2,1,0:T(4,128)S(1)} %bitcast.8) | data formatting | bytes 4096
